TPU v7x, 32 devices: a whole 2x2x4 slice. The times are simulated.
32 devices in a mesh: replica: 16 (over z, y, core), shard: 2 (over x).
Axes of the slice: x: 2, y: 2, z: 4, core: 2. Of those that a mesh axis runs over, the one named last changes fastest.
Arguments:
- tokens_in: bfloat16 [64, 256, 384], P('replica', 'shard'), may hold values from -6 to 6
- condition: bfloat16 [64, 384], P('replica'), may hold values from -6 to 6
- cotangent: bfloat16 [64, 256, 384], P('replica', 'shard'), may hold values from -6 to 6
- modulate_weight: bfloat16 [384, 2304], P('shard'), may hold values from -0.3125 to 0.3125
- modulate_bias: bfloat16 [2304], P('shard'), may hold values from -3 to 3
- attend_weight: bfloat16 [384, 1152], P('shard'), may hold values from -0.3125 to 0.3125
- query_value_bias: bfloat16 [768], P('shard'), may hold values from -3 to 3
- output_weight: bfloat16 [384, 384], P('shard'), may hold values from -2.5 to 2.5
- output_bias: bfloat16 [384], P('shard'), may hold values from -3 to 3
- widening_weight: bfloat16 [384, 1536], P('shard'), may hold values from -0.3125 to 0.3125
- widening_bias: bfloat16 [1536], P('shard'), may hold values from -3 to 3
- narrowing_weight: bfloat16 [1536, 384], P('shard'), may hold values from -0.15625 to 0.15625
- narrowing_bias: bfloat16 [384], P('shard'), may hold values from -3 to 3
Outputs:
- tokens_out: bfloat16 [64, 256, 384], P('replica', 'shard')
- grad_tokens: float32 [64, 256, 384], P('replica', 'shard')
- grad_condition: float32 [64, 384], P('replica')
- grad_modulate_weight: float32 [384, 2304], P('shard')
- grad_modulate_bias: float32 [2304], P('shard')
- grad_attend_weight: float32 [384, 1152], P('shard')
- grad_query_value_bias: float32 [768], P('shard')
- grad_output_weight: float32 [384, 384], P('shard')
- grad_output_bias: float32 [384], P('shard')
- grad_expand_weight: float32 [384, 1536], P('shard')
- grad_expand_bias: float32 [1536], P('shard')
- grad_shrink_weight: float32 [1536, 384], P('shard')
- grad_shrink_bias: float32 [384], P('shard')
All inputs are finite; a program needn't handle non-finite values.
Results may differ from a plain program's by a relative error of at most 0.01.
The roundings to bfloat16 on the way count: a program that leaves them out, or rounds other values in their place, can miss the bound.
Values may be sent and summed in bfloat16 or wider, within the bound.
A program may use at most 128 MiB of HBM per device.

v0:
```python
import jax
import jax.numpy as jnp
from jax import lax
from jax.sharding import PartitionSpec as P

D = 384
HEADS = 6
HEAD_DIM = 64


def modulate_norm(values, shift, scale):
    average = jnp.mean(values, axis=-1, keepdims=True)
    centered = values - average
    variance = jnp.mean(centered * centered, axis=-1, keepdims=True)
    return centered * lax.rsqrt(variance + 1e-06) * (1.0 + scale) + shift


def gelu_tanh(values):
    return jax.nn.gelu(values, approximate=True)


def on_device(
    tokens_in,
    condition,
    cotangent,
    modulate_weight,
    modulate_bias,
    attend_weight,
    query_value_bias,
    output_weight,
    output_bias,
    widening_weight,
    widening_bias,
    narrowing_weight,
    narrowing_bias,
):
    gathered = (
        lax.all_gather(modulate_weight, "shard", axis=0, tiled=True),
        lax.all_gather(modulate_bias, "shard", axis=0, tiled=True),
        lax.all_gather(attend_weight, "shard", axis=0, tiled=True),
        lax.all_gather(query_value_bias, "shard", axis=0, tiled=True),
        lax.all_gather(output_weight, "shard", axis=0, tiled=True),
        lax.all_gather(output_bias, "shard", axis=0, tiled=True),
        lax.all_gather(widening_weight, "shard", axis=0, tiled=True),
        lax.all_gather(widening_bias, "shard", axis=0, tiled=True),
        lax.all_gather(narrowing_weight, "shard", axis=0, tiled=True),
        lax.all_gather(narrowing_bias, "shard", axis=0, tiled=True),
    )
    w_modulate = gathered[0]
    b_modulate = gathered[1].astype(jnp.float32)
    w_attend = gathered[2]
    b_query_value = gathered[3].astype(jnp.float32)
    w_output = gathered[4]
    b_output = gathered[5].astype(jnp.float32)
    widening_matrix = gathered[6]
    b_expand = gathered[7].astype(jnp.float32)
    narrowing_matrix = gathered[8]
    b_shrink = gathered[9].astype(jnp.float32)
    parts = lax.axis_size("shard")
    rank = lax.axis_index("shard")
    score_scale = HEAD_DIM ** (-0.5)
    cond_float = condition.astype(jnp.float32)
    cond_act_all = jax.nn.silu(cond_float).astype(jnp.bfloat16)
    latents = tokens_in.shape[0]
    local_len = tokens_in.shape[1]
    tokens_float = tokens_in.astype(jnp.float32)
    modulation = jnp.dot(cond_act_all, w_modulate, preferred_element_type=jnp.float32) + b_modulate
    shift_one = modulation[:, None, 0:D]
    scale_one = modulation[:, None, D : 2 * D]
    gate_one = modulation[:, None, 2 * D : 3 * D]
    shift_two = modulation[:, None, 3 * D : 4 * D]
    scale_two = modulation[:, None, 4 * D : 5 * D]
    gate_two = modulation[:, None, 5 * D : 6 * D]
    normed_one = modulate_norm(tokens_float, shift_one, scale_one).astype(jnp.bfloat16)
    full_bias = jnp.concatenate(
        [b_query_value[:D], jnp.zeros((D,), jnp.float32), b_query_value[D:]]
    )
    projected = (
        jnp.einsum("lsd,de->lse", normed_one, w_attend, preferred_element_type=jnp.float32)
        + full_bias
    ).astype(jnp.bfloat16)
    keys_local = projected[..., D : 2 * D]
    values_local = projected[..., 2 * D :]
    keys_all, values_all = (
        lax.all_gather(keys_local, "shard", axis=1, tiled=True),
        lax.all_gather(values_local, "shard", axis=1, tiled=True),
    )
    seq_len = keys_all.shape[1]
    query_heads = projected[..., :D].reshape(latents, local_len, HEADS, HEAD_DIM)
    key_heads = keys_all.reshape(latents, seq_len, HEADS, HEAD_DIM)
    value_heads = values_all.reshape(latents, seq_len, HEADS, HEAD_DIM)
    scores = (
        jnp.einsum("lqhd,lkhd->lhqk", query_heads, key_heads, preferred_element_type=jnp.float32)
        * score_scale
    )
    highest = jnp.max(scores, axis=-1, keepdims=True)
    log_norm = highest + jnp.log(jnp.sum(jnp.exp(scores - highest), axis=-1, keepdims=True))
    probs_low = jnp.exp(scores - log_norm).astype(jnp.bfloat16)
    attended = jnp.einsum(
        "lhqk,lkhd->lqhd", probs_low, value_heads, preferred_element_type=jnp.float32
    )
    attended = attended.reshape(latents, local_len, D).astype(jnp.bfloat16)
    attn_out = (
        jnp.einsum("lsd,de->lse", attended, w_output, preferred_element_type=jnp.float32) + b_output
    )
    middle = tokens_float + gate_one * attn_out
    second_normalized = modulate_norm(middle, shift_two, scale_two).astype(jnp.bfloat16)
    hidden_preactivation = (
        jnp.einsum(
            "bei,ig->beg", second_normalized, widening_matrix, preferred_element_type=jnp.float32
        )
        + b_expand
    )
    hidden_activation = gelu_tanh(hidden_preactivation).astype(jnp.bfloat16)
    feedforward_output = (
        jnp.einsum(
            "ega,ap->egp", hidden_activation, narrowing_matrix, preferred_element_type=jnp.float32
        )
        + b_shrink
    )
    tokens_out = (middle + gate_two * feedforward_output).astype(jnp.bfloat16)
    backward_set = (
        lax.all_gather(modulate_weight, "shard", axis=0, tiled=True),
        lax.all_gather(modulate_bias, "shard", axis=0, tiled=True),
        lax.all_gather(attend_weight, "shard", axis=0, tiled=True),
        lax.all_gather(query_value_bias, "shard", axis=0, tiled=True),
        lax.all_gather(output_weight, "shard", axis=0, tiled=True),
        lax.all_gather(output_bias, "shard", axis=0, tiled=True),
        lax.all_gather(widening_weight, "shard", axis=0, tiled=True),
        lax.all_gather(widening_bias, "shard", axis=0, tiled=True),
        lax.all_gather(narrowing_weight, "shard", axis=0, tiled=True),
        lax.all_gather(narrowing_bias, "shard", axis=0, tiled=True),
    )
    back_modulate = backward_set[0]
    back_attend = backward_set[2]
    back_output = backward_set[4]
    expand_backward_pass = backward_set[6]
    shrink_backward_pass = backward_set[8]
    upstream = cotangent.astype(jnp.float32)
    feedforward_gradient = (gate_two * upstream).astype(jnp.bfloat16)
    d_gate_two = jnp.sum(upstream * feedforward_output, axis=1)
    narrowing_weight_gradient = jnp.einsum(
        "ukq,ukc->qc", hidden_activation, feedforward_gradient, preferred_element_type=jnp.float32
    )
    g_shrink_b = jnp.sum(feedforward_gradient.astype(jnp.float32), axis=(0, 1))
    activation_gradient = jnp.einsum(
        "het,jt->hej",
        feedforward_gradient,
        shrink_backward_pass,
        preferred_element_type=jnp.float32,
    )
    gelu_value, gelu_back = jax.vjp(gelu_tanh, hidden_preactivation)
    preactivation_gradient = gelu_back(activation_gradient)[0].astype(jnp.bfloat16)
    widening_weight_gradient = jnp.einsum(
        "mqo,mqz->oz", second_normalized, preactivation_gradient, preferred_element_type=jnp.float32
    )
    g_expand_b = jnp.sum(preactivation_gradient.astype(jnp.float32), axis=(0, 1))
    second_norm_gradient = jnp.einsum(
        "pkc,ac->pka",
        preactivation_gradient,
        expand_backward_pass,
        preferred_element_type=jnp.float32,
    )
    norm_value, norm_back = jax.vjp(modulate_norm, middle, shift_two, scale_two)
    d_mid_norm, d_shift_two, d_scale_two = norm_back(second_norm_gradient)
    d_middle = upstream + d_mid_norm
    d_attn = (gate_one * d_middle).astype(jnp.bfloat16)
    d_gate_one = jnp.sum(d_middle * attn_out, axis=1)
    g_output_w = jnp.einsum("lsd,lse->de", attended, d_attn, preferred_element_type=jnp.float32)
    g_output_b = jnp.sum(d_attn.astype(jnp.float32), axis=(0, 1))
    d_attended = jnp.einsum("lse,de->lsd", d_attn, back_output, preferred_element_type=jnp.float32)
    d_attended = d_attended.astype(jnp.bfloat16).reshape(latents, local_len, HEADS, HEAD_DIM)
    scores_again = (
        jnp.einsum("lqhd,lkhd->lhqk", query_heads, key_heads, preferred_element_type=jnp.float32)
        * score_scale
    )
    probs_again = jnp.exp(scores_again - log_norm)
    d_probs = jnp.einsum(
        "lqhd,lkhd->lhqk", d_attended, value_heads, preferred_element_type=jnp.float32
    )
    delta_sum = jnp.sum(probs_again * d_probs, axis=-1, keepdims=True)
    d_scores = (probs_again * (d_probs - delta_sum)).astype(jnp.bfloat16)
    d_values_all = jnp.einsum(
        "lhqk,lqhd->lkhd",
        probs_again.astype(jnp.bfloat16),
        d_attended,
        preferred_element_type=jnp.float32,
    )
    d_queries = (
        jnp.einsum("lhqk,lkhd->lqhd", d_scores, key_heads, preferred_element_type=jnp.float32)
        * score_scale
    )
    d_keys_all = (
        jnp.einsum("lhqk,lqhd->lkhd", d_scores, query_heads, preferred_element_type=jnp.float32)
        * score_scale
    )
    d_keys, d_values = (
        lax.psum_scatter(
            d_keys_all.reshape(latents, seq_len, D), "shard", scatter_dimension=1, tiled=True
        ),
        lax.psum_scatter(
            d_values_all.reshape(latents, seq_len, D), "shard", scatter_dimension=1, tiled=True
        ),
    )
    d_projected = jnp.concatenate(
        [d_queries.reshape(latents, local_len, D), d_keys, d_values], axis=-1
    ).astype(jnp.bfloat16)
    g_attend_w = jnp.einsum(
        "lsd,lse->de", normed_one, d_projected, preferred_element_type=jnp.float32
    )
    column_sums = jnp.sum(d_projected.astype(jnp.float32), axis=(0, 1))
    g_query_value = jnp.concatenate([column_sums[:D], column_sums[2 * D :]])
    d_norm_one = jnp.einsum(
        "lse,de->lsd", d_projected, back_attend, preferred_element_type=jnp.float32
    )
    norm_value, norm_back = jax.vjp(modulate_norm, tokens_float, shift_one, scale_one)
    d_in_norm, d_shift_one, d_scale_one = norm_back(d_norm_one)
    grad_work = d_middle + d_in_norm
    mod_partial = jnp.concatenate(
        [
            d_shift_one[:, 0],
            d_scale_one[:, 0],
            d_gate_one,
            d_shift_two[:, 0],
            d_scale_two[:, 0],
            d_gate_two,
        ],
        axis=-1,
    )
    mod_total = lax.psum(mod_partial, "shard")
    d_modulation = mod_total.astype(jnp.bfloat16)
    d_cond_act = jnp.einsum(
        "le,de->ld", d_modulation, back_modulate, preferred_element_type=jnp.float32
    )
    silu_value, silu_back = jax.vjp(jax.nn.silu, cond_float)
    grad_condition = silu_back(d_cond_act)[0]
    own_rows = D // parts
    own_act = lax.dynamic_slice_in_dim(cond_act_all, rank * own_rows, own_rows, 1)
    g_modulate_w = jnp.einsum(
        "lr,le->re", own_act, d_modulation, preferred_element_type=jnp.float32
    )
    bias_cols = 6 * D // parts
    g_modulate_b = lax.dynamic_slice_in_dim(
        jnp.sum(d_modulation.astype(jnp.float32), axis=0), rank * bias_cols, bias_cols, 0
    )
    owned = (
        lax.psum_scatter(g_attend_w, "shard", scatter_dimension=0, tiled=True),
        lax.psum_scatter(g_query_value, "shard", scatter_dimension=0, tiled=True),
        lax.psum_scatter(g_output_w, "shard", scatter_dimension=0, tiled=True),
        lax.psum_scatter(g_output_b, "shard", scatter_dimension=0, tiled=True),
        lax.psum_scatter(widening_weight_gradient, "shard", scatter_dimension=0, tiled=True),
        lax.psum_scatter(g_expand_b, "shard", scatter_dimension=0, tiled=True),
        lax.psum_scatter(narrowing_weight_gradient, "shard", scatter_dimension=0, tiled=True),
        lax.psum_scatter(g_shrink_b, "shard", scatter_dimension=0, tiled=True),
    )
    finals = lax.psum(
        (
            g_modulate_w,
            g_modulate_b,
            owned[0],
            owned[1],
            owned[2],
            owned[3],
            owned[4],
            owned[5],
            owned[6],
            owned[7],
        ),
        "replica",
    )
    return (
        tokens_out,
        grad_work,
        grad_condition,
        finals[0],
        finals[1],
        finals[2],
        finals[3],
        finals[4],
        finals[5],
        finals[6],
        finals[7],
        finals[8],
        finals[9],
    )


def solution(mesh):
    return jax.shard_map(
        on_device,
        mesh=mesh,
        in_specs=(
            P("replica", "shard", None),
            P("replica", None),
            P("replica", "shard", None),
            P("shard", None),
            P("shard"),
            P("shard", None),
            P("shard"),
            P("shard", None),
            P("shard"),
            P("shard", None),
            P("shard"),
            P("shard", None),
            P("shard"),
        ),
        out_specs=(
            P("replica", "shard", None),
            P("replica", "shard", None),
            P("replica", None),
            P("shard", None),
            P("shard"),
            P("shard", None),
            P("shard"),
            P("shard", None),
            P("shard"),
            P("shard", None),
            P("shard"),
            P("shard", None),
            P("shard"),
        ),
        check_vma=False,
    )
```

profile of v0, /device:TPU:0, one launch (start us, length us, event | category | flops | bytes accessed | tf_op | source)
XLA Modules:
  0.0 452.3 jit_solution(15443393570959819685)
XLA Ops:
  9.5 1.3 fusion.65
  13.2 5.8 %all-reduce.9 = (bf16[384]{0:T(512)(128)(2,1)S(1)}, bf16[384]{0:T(512)(128)(2,1)S(1)}) all-reduce(bf16[384]{0:T(512)(128)(2,1)S(1)} %dynamic-update-slice, bf16[384]{0:T(512)(128)(2,1)S(1)} %dynamic-update-slice.1), channel_id=1, replica_groups=mesh['replica'=16,'shard'=2] {'shard'}, use_global_device_ids=true, to_apply=%add | all-reduce | flops 768 | bytes 3072
  20.3 4.3 all-gather.1
  25.2 1.1 convert_reduce_fusion.2
  26.4 1.3 fusion.27
  28.9 4.4 all-gather.2
  34.6 4.4 all-gather
  39.1 5.9 %all_gather.47 = bf16[384,384]{1,0:T(8,128)(2,1)} all-gather(bf16[192,384]{1,0:T(8,128)(2,1)S(1)} %copy-done.26), channel_id=1, replica_groups=mesh['replica'=16,'shard'=2] {'shard'}, dimensions={0}, use_global_device_ids=true | all-gather | bytes 442368 | tf_op jit(solution)/shard_map/all_gather | solution.py:42
  45.1 14.2 %all_gather.43 = bf16[384,1152]{1,0:T(8,128)(2,1)S(1)} all-gather(bf16[192,1152]{1,0:T(8,128)(2,1)S(1)} %copy-done.22), channel_id=1, replica_groups=mesh['replica'=16,'shard'=2] {'shard'}, dimensions={0}, use_global_device_ids=true | all-gather | bytes 1327104 | tf_op jit(solution)/shard_map/all_gather | solution.py:40
  59.3 2.1 convolution_add_fusion.2
  63.7 13.6 %all_gather.46 = bf16[4,256,384]{2,1,0:T(8,128)(2,1)S(1)} all-gather(bf16[4,128,384]{2,1,0:T(8,128)(2,1)S(1)} %get-tuple-element.49), channel_id=1, replica_groups=mesh['replica'=16,'shard'=2] {'shard'}, dimensions={1}, use_global_device_ids=true | all-gather | bytes 1179648 | tf_op jit(solution)/shard_map/all_gather | solution.py:85
  77.3 1.2 copy.65
  79.4 14.9 %all_gather.45 = bf16[4,256,384]{2,1,0:T(8,128)(2,1)S(1)} all-gather(bf16[4,128,384]{2,1,0:T(8,128)(2,1)S(1)} %get-tuple-element.51), channel_id=1, replica_groups=mesh['replica'=16,'shard'=2] {'shard'}, dimensions={1}, use_global_device_ids=true | all-gather | bytes 1179648 | tf_op jit(solution)/shard_map/all_gather | solution.py:86
  94.3 1.2 copy.63
  95.4 2.0 multiply_reduce_fusion.1
  99.4 1.4 fusion.61
  103.1 4.2 convolution_add_fusion.1
  107.3 5.7 %convert_reduce_fusion = (f32[1536]{0:T(1024)}, bf16[4,128,1536]{2,1,0:T(8,128)(2,1)S(1)}) fusion(f32[4,128,1536]{2,1,0:T(8,128)} %convolution_add_fusion.1, bf16[1536,384]{1,0:T(8,128)(2,1)} %all-gather.11.cloned.1.call-done, bf16[4,128,384]{2,1,0:T(8,128)(2,1)} %param.15, f32[4,384]{1,0:T(4,128)} %get-tuple-element.53), kind=kOutput, calls=%fused_computation.12 | convolution fusion | flops 621869568 | bytes 6303744 | tf_op jit(solution)/shard_map/het,jt->hej/dot_general | solution.py:146
  113.2 1.7 multiply_reduce_fusion.2
  116.4 2.9 convert_reduce_fusion.3
  120.0 1.2 convolution_convert_fusion.1
  121.2 1.9 copy.67
  123.1 2.9 fusion.36
  126.0 3.0 copy.69
  129.3 2.5 multiply_reduce_fusion
  131.9 1.0 multiply_convert_fusion
  132.9 1.2 copy-done
  134.5 1.6 copy.68
  136.2 1.2 convolution_bitcast_fusion.3
  137.6 3.8 convolution_bitcast_fusion.1
  141.5 4.9 %convolution_bitcast_fusion = f32[1536,384]{1,0:T(8,128)} fusion(bf16[4,128,384]{2,1,0:T(8,128)(2,1)S(1)} %copy-done.24, f32[4,384]{1,0:T(4,128)S(1)} %copy-done.54, f32[4,128,1536]{2,1,0:T(8,128)} %convolution_add_fusion.1), kind=kOutput, calls=%fused_computation.19 | convolution fusion | flops 611647488 | bytes 5904384 | tf_op jit(solution)/shard_map/ukq,ukc->qc/dot_general | solution.py:142
  147.4 6.8 %reduce-scatter.9.cloned.1.call-done = f32[4,128,384]{2,1,0:T(8,128)} async-done(((f32[4,256,384]{2,1,0:T(8,128)}), f32[4,128,384]{2,1,0:T(8,128)}) %reduce-scatter.9.cloned.1.call-update) | async-done | bytes 786448 | tf_op jit(solution)/shard_map/reduce_scatter | solution.py:201
  154.3 1.2 convert.13
  155.4 27.7 %reduce-scatter.7.cloned.1.call-done = f32[4,128,384]{2,1,0:T(8,128)} async-done(((f32[4,256,384]{2,1,0:T(8,128)}), f32[4,128,384]{2,1,0:T(8,128)}) %reduce-scatter.7.cloned.1.call-update) | async-done | bytes 786448 | tf_op jit(solution)/shard_map/reduce_scatter | solution.py:198
  183.1 1.2 convert.12
  184.3 2.8 convolution_bitcast_fusion.2
  187.5 2.1 fusion.28
  190.3 8.6 %all-reduce.8 = (bf16[4,2304]{1,0:T(4,128)(2,1)S(1)}, f32[768]{0:T(1024)S(1)}, f32[384]{0:T(512)S(1)}, f32[1536]{0:T(1024)S(1)}, f32[384]{0:T(512)S(1)}) all-reduce(f32[4,2304]{1,0:T(4,128)S(1)} %constant_dynamic-update-slice_fusion, f32[768]{0:T(1024)S(1)} %pad_maximum_fusion.2, ...), channel_id=1, replica_groups=mesh['replica'=16,'shard'=2] {'shard'}, use_global_device_ids=true, to_apply=%region_19.20 | all-reduce | flops 12288 | bytes 79872 | tf_op jit(solution)/shard_map/psum | solution.py:230
  199.0 1.7 fusion.47
  200.7 1.7 reduce-scatter.13.cloned.1.call-done
  202.4 37.1 %reduce-scatter.15.cloned.1.call-done = f32[192,1536]{1,0:T(8,128)} async-done(((f32[384,1536]{1,0:T(8,128)}), f32[192,1536]{1,0:T(8,128)}) %reduce-scatter.15.cloned.1.call-update) | async-done | bytes 1179664 | tf_op jit(solution)/shard_map/reduce_scatter | solution.py:251
  239.4 37.0 %reduce-scatter.17.cloned.1.call-done = f32[768,384]{1,0:T(8,128)} async-done(((f32[1536,384]{1,0:T(8,128)}), f32[768,384]{1,0:T(8,128)}) %reduce-scatter.17.cloned.1.call-update) | async-done | bytes 1179664 | tf_op jit(solution)/shard_map/reduce_scatter | solution.py:253
  276.4 30.6 %reduce-scatter.11.cloned.1.call-done = f32[192,1152]{1,0:T(8,128)} async-done(((f32[384,1152]{1,0:T(8,128)}), f32[192,1152]{1,0:T(8,128)}) %reduce-scatter.11.cloned.1.call-update) | async-done | bytes 884752 | tf_op jit(solution)/shard_map/reduce_scatter | solution.py:247
  309.5 63.6 %all-reduce.6 = (f32[1152]{0:T(1024)}, f32[384]{0:T(512)}, f32[192]{0:T(256)}, f32[768]{0:T(1024)}, f32[192]{0:T(256)}) all-reduce(f32[1152]{0:T(1024)S(1)} %dynamic_slice.7, f32[384]{0:T(512)S(1)} %dynamic-slice.3, f32[192]{0:T(256)S(1)} %dynamic-slice.5, ...), channel_id=1, replica_groups=mesh['replica'=16,'shard'=2] {'replica'}, use_global_device_ids=true, to_apply=%region_22.23 | all-reduce | flops 2688 | bytes 21504 | tf_op jit(solution)/shard_map/psum | solution.py:256
  373.1 1.2 fusion.46
  374.3 2.4 add_add_fusion.2
  376.7 62.1 %all-reduce.12.cloned.1.call-done = (f32[192,2304]{1,0:T(8,128)}, f32[192,1152]{1,0:T(8,128)}, f32[192,384]{1,0:T(8,128)}, f32[192,1536]{1,0:T(8,128)}, f32[768,384]{1,0:T(8,128)}) async-done(((f32[192,2304]{1,0:T(8,128)}, f32[192,1152]{1,0:T(8,128)}, f32[192,384]{1,0:T(8,128)}, f32[192,1536]{1,0:T(8,128)}, f32[768,384]{1,0:T(8,128)}), (f32[192,2304]{1,0:T(8,128)}, f32[192,1152]{1,0:T(8,128)}, ...) | async-done | bytes 5308432 | tf_op jit(solution)/shard_map/psum | solution.py:256
  438.8 2.9 copy.90
  (214 shorter events, 24.9 us)
Async XLA Ops:
  7.2 31.9 %copy-start.26 = (bf16[192,384]{1,0:T(8,128)(2,1)S(1)}, bf16[192,384]{1,0:T(8,128)(2,1)}, u32[]{:S(2)}) copy-start(bf16[192,384]{1,0:T(8,128)(2,1)} %param.20) | copy-start | bytes 442372
  7.2 37.9 %copy-start.22 = (bf16[192,1152]{1,0:T(8,128)(2,1)S(1)}, bf16[192,1152]{1,0:T(8,128)(2,1)}, u32[]{:S(2)}) copy-start(bf16[192,1152]{1,0:T(8,128)(2,1)} %param.18) | copy-start | bytes 1327108
  7.2 52.1 %copy-start.31 = (bf16[4,384]{1,0:T(4,128)(2,1)S(1)}, bf16[4,384]{1,0:T(4,128)(2,1)}, u32[]{:S(2)}) copy-start(bf16[4,384]{1,0:T(4,128)(2,1)} %param.14) | copy-start | bytes 9220
  7.2 52.0 %all-gather.7.cloned.1.call-start = ((), (), s32[]{:S(2)}) async-start(), calls=%async_computation.6 | async-start | bytes 2654208 | tf_op jit(solution)/shard_map/all_gather | solution.py:38
  7.9 54.7 %copy-start.2 = (bf16[4,128,384]{2,1,0:T(8,128)(2,1)S(1)}, bf16[4,128,384]{2,1,0:T(8,128)(2,1)}, u32[]{:S(2)}) copy-start(bf16[4,128,384]{2,1,0:T(8,128)(2,1)} %param.13) | copy-start | bytes 1179652
  8.0 95.1 %all-gather.9.cloned.1.call-start = ((), (), s32[]{:S(2)}) async-start(), calls=%async_computation.7 | async-start | bytes 1769472 | tf_op jit(solution)/shard_map/all_gather | solution.py:44
  8.7 98.6 %all-gather.11.cloned.1.call-start = ((), (), s32[]{:S(2)}) async-start(), calls=%async_computation.8 | async-start | bytes 1769472 | tf_op jit(solution)/shard_map/all_gather | solution.py:46
  9.4 144.8 %reduce-scatter.9.cloned.1.call-start = ((), (), s32[]{:S(2)}) async-start(), calls=%async_computation.10 | async-start | bytes 2359296 | tf_op jit(solution)/shard_map/reduce_scatter | solution.py:201
  26.4 35.6 %copy-start.29 = (f32[4,128]{1,0:T(4,128)}, f32[4,128]{1,0:T(4,128)S(1)}, u32[]{:S(2)}) copy-start(f32[4,128]{1,0:T(4,128)S(1)} %broadcast_multiply_fusion.1) | copy-start | bytes 6148
  28.2 33.8 %copy-start.37 = (f32[4,128]{1,0:T(4,128)}, f32[4,128]{1,0:T(4,128)S(1)}, u32[]{:S(2)}) copy-start(f32[4,128]{1,0:T(4,128)S(1)} %fusion.49) | copy-start | bytes 6148
  59.2 2.8 copy-start.20
  95.4 3.1 copy-start.7
  107.3 5.8 %copy-start.5 = (f32[4,128,384]{2,1,0:T(8,128)S(1)}, f32[4,128,384]{2,1,0:T(8,128)}, u32[]{:S(2)}) copy-start(f32[4,128,384]{2,1,0:T(8,128)} %copy-done.4) | copy-start | bytes 2359300
  107.3 5.8 %copy-start.35 = (f32[4,384]{1,0:T(4,128)S(1)}, f32[4,384]{1,0:T(4,128)}, u32[]{:S(2)}) copy-start(f32[4,384]{1,0:T(4,128)} %get-tuple-element.55) | copy-start | bytes 18436
  107.3 5.8 %copy-start.44 = (f32[4,128]{1,0:T(4,128)S(1)}, f32[4,128]{1,0:T(4,128)}, u32[]{:S(2)}) copy-start(f32[4,128]{1,0:T(4,128)} %copy-done.43) | copy-start | bytes 6148
  107.3 5.8 %copy-start.50 = (f32[4,128]{1,0:T(4,128)S(1)}, f32[4,128]{1,0:T(4,128)}, u32[]{:S(2)}) copy-start(f32[4,128]{1,0:T(4,128)} %fusion.50) | copy-start | bytes 6148
  107.3 5.8 %copy-start.64 = (bf16[384,1536]{1,0:T(8,128)(2,1)S(1)}, bf16[384,1536]{1,0:T(8,128)(2,1)}, u32[]{:S(2)}) copy-start(bf16[384,1536]{1,0:T(8,128)(2,1)} %all-gather.9.cloned.1.call-done) | copy-start | bytes 3538948
  113.2 3.2 copy-start.65
  115.3 4.0 copy-start.12
  115.3 4.0 copy-start.46
  116.4 3.6 copy-start.14
  129.0 54.1 %reduce-scatter.7.cloned.1.call-start = ((), (), s32[]{:S(2)}) async-start(), calls=%async_computation.9 | async-start | bytes 2359296 | tf_op jit(solution)/shard_map/reduce_scatter | solution.py:198
  134.5 3.0 copy-start.6
  134.5 3.0 copy-start.36
  134.5 3.0 copy-start.45
  134.5 3.0 copy-start.51
  136.2 66.2 %reduce-scatter.13.cloned.1.call-start = ((), (), s32[]{:S(2)}) async-start(), calls=%async_computation.12 | async-start | bytes 884736 | tf_op jit(solution)/shard_map/reduce_scatter | solution.py:249
  137.5 4.1 copy-start.24
  137.5 4.1 copy-start.54
  137.5 102.0 %reduce-scatter.15.cloned.1.call-start = ((), (), s32[]{:S(2)}) async-start(), calls=%async_computation.13 | async-start | bytes 3538944 | tf_op jit(solution)/shard_map/reduce_scatter | solution.py:251
  141.4 5.1 %copy-start.1 = (bf16[4,6,128,256]{3,2,1,0:T(8,128)(2,1)S(1)}, bf16[4,6,128,256]{3,2,1,0:T(8,128)(2,1)}, u32[]{:S(2)}) copy-start(bf16[4,6,128,256]{3,2,1,0:T(8,128)(2,1)} %copy-done) | copy-start | bytes 4718596
  141.5 5.1 %copy-start.8 = (bf16[4,256,384]{1,2,0:T(8,128)(2,1)S(1)}, bf16[4,256,384]{1,2,0:T(8,128)(2,1)}, u32[]{:S(2)}) copy-start(bf16[4,256,384]{1,2,0:T(8,128)(2,1)} %copy.65) | copy-start | bytes 2359300
  141.5 135.0 %reduce-scatter.17.cloned.1.call-start = ((), (), s32[]{:S(2)}) async-start(), calls=%async_computation.14 | async-start | bytes 3538944 | tf_op jit(solution)/shard_map/reduce_scatter | solution.py:253
  146.4 37.9 %copy-start.28 = (f32[4,384]{1,0:T(4,128)S(1)}, f32[4,384]{1,0:T(4,128)}, u32[]{:S(2)}) copy-start(f32[4,384]{1,0:T(4,128)} %copy-done.27) | copy-start | bytes 18436
  146.4 37.9 %copy-start.30 = (f32[4,128]{1,0:T(4,128)S(1)}, f32[4,128]{1,0:T(4,128)}, u32[]{:S(2)}) copy-start(f32[4,128]{1,0:T(4,128)} %copy-done.29) | copy-start | bytes 6148
  146.4 37.9 %copy-start.38 = (f32[4,128]{1,0:T(4,128)S(1)}, f32[4,128]{1,0:T(4,128)}, u32[]{:S(2)}) copy-start(f32[4,128]{1,0:T(4,128)} %copy-done.37) | copy-start | bytes 6148
  146.5 160.6 %reduce-scatter.11.cloned.1.call-start = ((), (), s32[]{:S(2)}) async-start(), calls=%async_computation.11 | async-start | bytes 2654208 | tf_op jit(solution)/shard_map/reduce_scatter | solution.py:247
  184.3 2.9 copy-start.32
  187.1 251.7 %all-reduce.12.cloned.1.call-start = ((), (), s32[]{:S(2)}) async-start(), calls=%async_computation.15 | async-start | bytes 10616832 | tf_op jit(solution)/shard_map/psum | solution.py:256
  187.5 2.8 copy-start.58
  187.5 2.8 copy-start.49
  187.5 2.8 copy-start.61
  187.5 2.8 copy-start.62
  200.7 172.4 %copy-start.3 = (bf16[384,2304]{1,0:T(8,128)(2,1)S(1)}, bf16[384,2304]{1,0:T(8,128)(2,1)}, u32[]{:S(2)}) copy-start(bf16[384,2304]{1,0:T(8,128)(2,1)} %all-gather.7.cloned.1.call-done) | copy-start | bytes 5308420
  307.1 67.2 %copy-start.47 = (f32[4,128]{1,0:T(4,128)S(1)}, f32[4,128]{1,0:T(4,128)}, u32[]{:S(2)}) copy-start(f32[4,128]{1,0:T(4,128)} %copy-done.46) | copy-start | bytes 6148
  438.8 3.0 copy-start.19
  438.8 3.9 copy-start.25
  438.8 4.6 %copy-start.18 = (f32[192,1536]{1,0:T(8,128)S(1)}, f32[192,1536]{1,0:T(8,128)}, u32[]{:S(2)}) copy-start(f32[192,1536]{1,0:T(8,128)} %get-tuple-element.82) | copy-start | bytes 3538948
  (29 other events, 52.0 us)
Sparse Core Ops, SparseCore 0:
  9.6 33.8 all-gather.6
  45.0 29.3 all-gather.8
  75.9 26.1 all-gather.10
  129.2 25.0 reduce-scatter.8
  157.0 26.0 reduce-scatter.6
  185.8 16.5 reduce-scatter.12
  204.7 34.6 reduce-scatter.14
  241.7 34.7 reduce-scatter.16
  278.8 28.2 reduce-scatter.10
  311.7 127.0 all-reduce.11
where the time goes:
time: 453 us; the launch traced here: 452 us
  waiting for transfers between devices  205 us (45%)
  blocking collectives  140 us (31%)
  matrix products  47 us (10%)
  local copies, waits for them, and re-layouts  28.7 us (6%)
  between operations  17.7 us (4%)
  other arithmetic  13.2 us (3%)
    psum x1, blocking collectives, on_device(): lax.psum((g_modulate_w, g_modulate_b, owned[0], owned[1], owned[2], owned...  63.6 us
    psum x1, waiting for transfers between devices, on_device(): lax.psum((g_modulate_w, g_modulate_b, owned[0], owned[1], owned[2], owned...  62.1 us
    reduce_scatter x1, waiting for transfers between devices, on_device(): lax.psum_scatter(widening_weight_gradient, 'shard', scatter_dimension=0,...  37.1 us
    reduce_scatter x1, waiting for transfers between devices, on_device(): lax.psum_scatter(narrowing_weight_gradient, 'shard', scatter_dimension=0,...  37 us
    reduce_scatter x1, waiting for transfers between devices, on_device(): lax.psum_scatter(g_attend_w, 'shard', scatter_dimension=0, tiled=True)  30.6 us
    reduce_scatter x1, waiting for transfers between devices, on_device(): lax.psum_scatter(d_keys_all.reshape(latents, seq_len, D), 'shard', scatte...  27.7 us
    unnamed x156, local copies, waits for them, and re-layouts  17.8 us
    all_gather x1, blocking collectives, on_device(): lax.all_gather(values_local, 'shard', axis=1, tiled=True)  14.9 us
  transfers between devices with their start and end apart: 10, of which 7 were waited for; matrix products, arithmetic and copies ran while one was open for 13% of the time, Pallas kernels for 0%

commit v1 on v0

v1 whole, which is shorter than its diff:
```python
import functools
import jax
import jax.numpy as jnp
from jax import lax
from jax.experimental import pallas as pl
from jax.experimental.pallas import tpu as pltpu
from jax.sharding import PartitionSpec as P

D = 384
HEADS = 6
HEAD_DIM = 64
FF = 1536
CHUNKS = 3
ROWS = 768
BLOCK_ROWS = 80
F32 = jnp.float32
BF16 = jnp.bfloat16
SWAP = [(0, 1), (1, 0)]


def modulate_norm(values, shift, scale):
    average = jnp.mean(values, axis=-1, keepdims=True)
    centered = values - average
    variance = jnp.mean(centered * centered, axis=-1, keepdims=True)
    return centered * lax.rsqrt(variance + 1e-06) * (1.0 + scale) + shift


def gelu_tanh(values):
    return jax.nn.gelu(values, approximate=True)


def flip(index, bit):
    step = 1 << bit
    return index + step - 2 * step * ((index // step) % 2)


def bit_of(index, bit):
    return (index // (1 << bit)) % 2


def greet(partners):
    barrier = pltpu.get_barrier_semaphore()
    for partner in partners:
        pl.semaphore_signal(barrier, inc=1, device_id=partner, device_id_type=pl.DeviceIdType.MESH)
    pl.semaphore_wait(barrier, len(partners))


def gather_kernel(
    tok, cot, small, wa, wo, ww, wn,
    tok_all, cot_all, small_other, wa_all, wo_all, ww_all, wn_all,
    send_one, recv_one, send_w, recv_w, local_sem,
):
    r, s = lax.axis_index("replica"), lax.axis_index("shard")
    o = 1 - s
    over_x, over_core, over_y = (r, o), (flip(r, 0), s), (flip(r, 1), s)
    greet((over_x, over_core, over_y))

    def remote(src, dst, send, recv, device):
        copy = pltpu.make_async_remote_copy(
            src_ref=src, dst_ref=dst, send_sem=send, recv_sem=recv,
            device_id=device, device_id_type=pl.DeviceIdType.MESH,
        )
        return copy

    length = tok.shape[1]
    group = tok.shape[0] // 2
    place = pl.ds(pl.multiple_of(s * length, length), length)

    def exchange(src, dst, k):
        return remote(
            src.at[pl.ds(o * group, group)], dst.at[:, place], send_one.at[k], recv_one.at[k], over_x
        )

    swaps = [
        remote(small, small_other, send_one.at[0], recv_one.at[0], over_x),
        exchange(tok, tok_all, 1),
        exchange(cot, cot_all, 2),
    ]
    swaps[0].start()
    swaps[1].start()

    pairs = ((wa, wa_all), (wo, wo_all), (ww, ww_all), (wn, wn_all))
    quarter = r % 4

    def rows_at(full, half, q):
        n = full.shape[0] // 8
        return full.at[pl.ds(pl.multiple_of(half * (4 * n) + q * n, n), n)]

    first = []
    for k, (own, full) in enumerate(pairs):
        n = own.shape[0] // 4
        c = remote(
            own.at[pl.ds(pl.multiple_of(quarter * n, n), n)], rows_at(full, s, quarter),
            send_w.at[k, 0], recv_w.at[k, 0], over_x,
        )
        c.start()
        first.append(c)
    swaps[2].start()
    locals_ = []
    for k, (src, dst) in enumerate(((tok, tok_all), (cot, cot_all))):
        locals_.append(
            pltpu.make_async_copy(src.at[pl.ds(s * group, group)], dst.at[:, place], local_sem.at[k])
        )
    for k, (own, full) in enumerate(pairs):
        n = own.shape[0]
        locals_.append(
            pltpu.make_async_copy(own, full.at[pl.ds(pl.multiple_of(s * n, n), n)], local_sem.at[2 + k])
        )
    for c in locals_:
        c.start()
    later = []
    for k, (own, full) in enumerate(pairs):
        first[k].wait_recv()
        mine = rows_at(full, o, quarter)
        by_y = remote(mine, mine, send_w.at[k, 1], recv_w.at[k, 1], over_y)
        by_y.start()
        by_core = remote(mine, mine, send_w.at[k, 2], recv_w.at[k, 2], over_core)
        by_core.start()
        later.append((by_y, by_core))
    last = []
    for k, (own, full) in enumerate(pairs):
        later[k][0].wait_recv()
        came = rows_at(full, o, flip(quarter, 1))
        c = remote(came, came, send_w.at[k, 3], recv_w.at[k, 3], over_core)
        c.start()
        last.append(c)
    for k in range(4):
        later[k][1].wait_recv()
        last[k].wait_recv()
    for c in swaps:
        c.wait_recv()
    for c in locals_:
        c.wait()
    for c in swaps + first + last:
        c.wait_send()
    for a, b in later:
        a.wait_send()
        b.wait_send()


def gather_all(tok, cot, small, wa, wo, ww, wn):
    any_spec = pl.BlockSpec(memory_space=pl.ANY)
    group = tok.shape[0] // 2

    def full(w):
        return jax.ShapeDtypeStruct((w.shape[0] * 2, w.shape[1]), w.dtype)

    tokens = jax.ShapeDtypeStruct((group, 2 * tok.shape[1], D), BF16)
    return pl.pallas_call(
        gather_kernel,
        out_shape=(
            tokens, tokens, jax.ShapeDtypeStruct(small.shape, small.dtype),
            full(wa), full(wo), full(ww), full(wn),
        ),
        in_specs=[any_spec] * 7,
        out_specs=(any_spec,) * 7,
        scratch_shapes=[
            pltpu.SemaphoreType.DMA((3,)),
            pltpu.SemaphoreType.DMA((3,)),
            pltpu.SemaphoreType.DMA((4, 4)),
            pltpu.SemaphoreType.DMA((4, 4)),
            pltpu.SemaphoreType.DMA((6,)),
        ],
        compiler_params=pltpu.CompilerParams(collective_id=0, has_side_effects=True),
    )(tok, cot, small, wa, wo, ww, wn)


def reduce_kernel(
    bits, grads, block, out, blocks,
    core_in, x_out, x_in, total, half_out, half_in, extra_out, extra_in,
    send_sem, recv_sem, send_blk, recv_blk, local_sem,
):
    r, s = lax.axis_index("replica"), lax.axis_index("shard")
    o = 1 - s
    over_x = (r, o)
    over = [(flip(r, k), s) for k in range(bits)]
    greet([over_x] + over)
    core = bit_of(r, 0)

    def remote(src, dst, send, recv, device):
        copy = pltpu.make_async_remote_copy(
            src_ref=src, dst_ref=dst, send_sem=send, recv_sem=recv,
            device_id=device, device_id_type=pl.DeviceIdType.MESH,
        )
        copy.start()
        return copy

    pending = []

    order = [(over[k], bit_of(r, k)) for k in range(bits - 1, 0, -1)]
    order += [(over_x, s), (over[0], core)]
    index = sum(b * (1 << k) for k, (_, b) in enumerate(order))
    own_block = pltpu.make_async_copy(block, blocks.at[index], local_sem)
    own_block.start()

    def gather_steps():
        own_block.wait()
        for k, (device, _) in enumerate(order):
            count = 1 << k
            start = (index // count) * count
            part = blocks.at[pl.ds(start, count)]
            c = remote(part, part, send_blk.at[k], recv_blk.at[k], device)
            pending.append(c)
            yield
            c.wait_recv()

    def rows(n, start):
        return pl.ds(pl.multiple_of(start, 16), n)

    def chunk_steps(j):
        base = j * ROWS
        half = ROWS // 2
        away = rows(half, base + (1 - core) * half)
        kept = rows(half, base + core * half)
        c = remote(grads.at[:, away], core_in.at[j], send_sem.at[j, 0], recv_sem.at[j, 0], over[0])
        pending.append(c)
        yield
        c.wait_recv()
        x_out[j] = (grads[o, kept].astype(F32) + core_in[j, o].astype(F32)).astype(BF16)
        c = remote(x_out.at[j], x_in.at[j], send_sem.at[j, 1], recv_sem.at[j, 1], over_x)
        pending.append(c)
        total[j] = grads[s, kept].astype(F32) + core_in[j, s].astype(F32)
        yield
        c.wait_recv()
        total[j] += x_in[j].astype(F32)
        n, start, at = half // 2, 0, 0
        for k in (1, 2, 3):
            b = bit_of(r, k)
            spot = rows(n, at)
            half_out[j, spot] = total[j, rows(n, start + (1 - b) * n)].astype(BF16)
            c = remote(
                half_out.at[j, spot], half_in.at[j, spot],
                send_sem.at[j, 1 + k], recv_sem.at[j, 1 + k], over[k],
            )
            pending.append(c)
            yield
            c.wait_recv()
            start = start + b * n
            total[j, rows(n, start)] += half_in[j, spot].astype(F32)
            at += n
            n //= 2
        n *= 2
        for e in range(bits - 4):
            extra_out[j, e] = total[j, rows(n, start)].astype(BF16)
            c = remote(
                extra_out.at[j, e], extra_in.at[j, e],
                send_sem.at[j, 9 + e], recv_sem.at[j, 9 + e], over[4 + e],
            )
            pending.append(c)
            yield
            c.wait_recv()
            total[j, rows(n, start)] += extra_in[j, e].astype(F32)
        spot = base + core * half + start
        out[rows(n, spot)] = total[j, rows(n, start)].astype(BF16)
        for step, k in enumerate((3, 2, 1, 0)):
            part = out.at[rows(n, spot)]
            c = remote(part, part, send_sem.at[j, 5 + step], recv_sem.at[j, 5 + step], over[k])
            pending.append(c)
            yield
            c.wait_recv()
            spot = spot - bit_of(r, k) * n
            n *= 2

    waiting = [chunk_steps(j) for j in range(CHUNKS)]
    running = [gather_steps()]
    while running or waiting:
        if waiting:
            running.append(waiting.pop(0))
        for steps in list(running):
            if next(steps, 0) == 0:
                running.remove(steps)
    for c in pending:
        c.wait_send()


def reduce_all(grads, block, replicas):
    bits = replicas.bit_length() - 1
    extra = max(bits - 4, 1)
    vmem = pl.BlockSpec(memory_space=pltpu.VMEM)
    half = ROWS // 2
    return pl.pallas_call(
        functools.partial(reduce_kernel, bits),
        out_shape=(
            jax.ShapeDtypeStruct((CHUNKS * ROWS, D), BF16),
            jax.ShapeDtypeStruct((2 * replicas, BLOCK_ROWS, 128), BF16),
        ),
        in_specs=[vmem, vmem],
        out_specs=(vmem, vmem),
        scratch_shapes=[
            pltpu.VMEM((CHUNKS, 2, half, D), BF16),
            pltpu.VMEM((CHUNKS, half, D), BF16),
            pltpu.VMEM((CHUNKS, half, D), BF16),
            pltpu.VMEM((CHUNKS, half, D), F32),
            pltpu.VMEM((CHUNKS, half, D), BF16),
            pltpu.VMEM((CHUNKS, half, D), BF16),
            pltpu.VMEM((CHUNKS, extra, half // 8, D), BF16),
            pltpu.VMEM((CHUNKS, extra, half // 8, D), BF16),
            pltpu.SemaphoreType.DMA((CHUNKS, 9 + extra)),
            pltpu.SemaphoreType.DMA((CHUNKS, 9 + extra)),
            pltpu.SemaphoreType.DMA((bits + 1,)),
            pltpu.SemaphoreType.DMA((bits + 1,)),
            pltpu.SemaphoreType.DMA,
        ],
        compiler_params=pltpu.CompilerParams(
            collective_id=1, has_side_effects=True, vmem_limit_bytes=48 * 2**20
        ),
    )(grads, block)


def in_halves(gradient):
    rows = gradient.shape[0] // 2
    columns = [gradient[:, i : i + D].reshape(2, rows, D) for i in range(0, gradient.shape[1], D)]
    return jnp.concatenate(columns, axis=1) if len(columns) > 1 else columns[0]


def on_device(
    tokens_in,
    condition,
    cotangent,
    modulate_weight,
    modulate_bias,
    attend_weight,
    query_value_bias,
    output_weight,
    output_bias,
    widening_weight,
    widening_bias,
    narrowing_weight,
    narrowing_bias,
):
    rank = lax.axis_index("shard")
    replicas = lax.axis_size("replica")
    score_scale = HEAD_DIM ** (-0.5)
    latents = tokens_in.shape[0] // 2
    local_len = tokens_in.shape[1]
    seq_len = 2 * local_len
    own_rows = D // 2
    cond_float = condition.astype(F32)
    cond_act_all = jax.nn.silu(cond_float).astype(BF16)
    own_act = lax.dynamic_slice_in_dim(cond_act_all, rank * own_rows, own_rows, 1)
    mod_part = jnp.dot(own_act, modulate_weight, preferred_element_type=F32)
    mod_keep = lax.dynamic_slice_in_dim(mod_part, rank * latents, latents, 0)
    mod_send = lax.dynamic_slice_in_dim(mod_part, (1 - rank) * latents, latents, 0)
    biases = jnp.concatenate(
        [modulate_bias, query_value_bias, output_bias, widening_bias, narrowing_bias]
    ).astype(F32)
    sent = jnp.concatenate([mod_send.reshape(-1), biases])
    pad = (-sent.shape[0]) % 1024
    small = jnp.pad(sent, (0, pad)).reshape(-1, 128)
    tokens_in, cotangent, small_other, w_attend, w_output, widening_matrix, narrowing_matrix = (
        gather_all(
            tokens_in, cotangent, small, attend_weight, output_weight, widening_weight, narrowing_weight
        )
    )
    small_other = small_other.reshape(-1)
    count = latents * 6 * D
    mod_other = small_other[:count].reshape(latents, 6 * D)
    bias_other = small_other[count : count + biases.shape[0]]

    def both(start, size):
        own, other = biases[start : start + size], bias_other[start : start + size]
        return jnp.where(
            rank == 0, jnp.concatenate([own, other]), jnp.concatenate([other, own])
        )

    b_modulate = both(0, 3 * D)
    b_query_value = both(3 * D, D)
    b_output = both(4 * D, D // 2)
    b_expand = both(4 * D + D // 2, FF // 2)
    b_shrink = both(4 * D + D // 2 + FF // 2, D // 2)

    tokens_float = tokens_in.astype(F32)
    modulation = mod_keep + mod_other + b_modulate
    shift_one = modulation[:, None, 0:D]
    scale_one = modulation[:, None, D : 2 * D]
    gate_one = modulation[:, None, 2 * D : 3 * D]
    shift_two = modulation[:, None, 3 * D : 4 * D]
    scale_two = modulation[:, None, 4 * D : 5 * D]
    gate_two = modulation[:, None, 5 * D : 6 * D]
    normed_one = modulate_norm(tokens_float, shift_one, scale_one).astype(BF16)
    full_bias = jnp.concatenate([b_query_value[:D], jnp.zeros((D,), F32), b_query_value[D:]])
    projected = (
        jnp.einsum("lsd,de->lse", normed_one, w_attend, preferred_element_type=F32) + full_bias
    ).astype(BF16)
    query_heads = projected[..., :D].reshape(latents, seq_len, HEADS, HEAD_DIM)
    key_heads = projected[..., D : 2 * D].reshape(latents, seq_len, HEADS, HEAD_DIM)
    value_heads = projected[..., 2 * D :].reshape(latents, seq_len, HEADS, HEAD_DIM)
    scores = (
        jnp.einsum("lqhd,lkhd->lhqk", query_heads, key_heads, preferred_element_type=F32)
        * score_scale
    )
    highest = jnp.max(scores, axis=-1, keepdims=True)
    log_norm = highest + jnp.log(jnp.sum(jnp.exp(scores - highest), axis=-1, keepdims=True))
    probs = jnp.exp(scores - log_norm)
    probs_low = probs.astype(BF16)
    attended = jnp.einsum("lhqk,lkhd->lqhd", probs_low, value_heads, preferred_element_type=F32)
    attended = attended.reshape(latents, seq_len, D).astype(BF16)
    attn_out = jnp.einsum("lsd,de->lse", attended, w_output, preferred_element_type=F32) + b_output
    middle = tokens_float + gate_one * attn_out
    second_normalized = modulate_norm(middle, shift_two, scale_two).astype(BF16)
    hidden_pre = (
        jnp.einsum("bei,ig->beg", second_normalized, widening_matrix, preferred_element_type=F32)
        + b_expand
    )
    hidden_act = gelu_tanh(hidden_pre).astype(BF16)
    mlp_out = (
        jnp.einsum("ega,ap->egp", hidden_act, narrowing_matrix, preferred_element_type=F32) + b_shrink
    )
    tokens_out = (middle + gate_two * mlp_out).astype(BF16)

    upstream = cotangent.astype(F32)
    d_mlp = (gate_two * upstream).astype(BF16)
    d_gate_two = jnp.sum(upstream * mlp_out, axis=1)
    g_shrink_w = jnp.einsum("ukq,ukc->qc", hidden_act, d_mlp, preferred_element_type=F32)
    g_shrink_b = jnp.sum(d_mlp.astype(F32), axis=(0, 1))
    d_act = jnp.einsum("het,jt->hej", d_mlp, narrowing_matrix, preferred_element_type=F32)
    _, gelu_back = jax.vjp(gelu_tanh, hidden_pre)
    d_pre = gelu_back(d_act)[0].astype(BF16)
    g_expand_w = jnp.einsum("mqo,mqz->oz", second_normalized, d_pre, preferred_element_type=F32)
    g_expand_b = jnp.sum(d_pre.astype(F32), axis=(0, 1))
    d_second = jnp.einsum("pkc,ac->pka", d_pre, widening_matrix, preferred_element_type=F32)
    _, norm_back = jax.vjp(modulate_norm, middle, shift_two, scale_two)
    d_mid_norm, d_shift_two, d_scale_two = norm_back(d_second)
    d_middle = upstream + d_mid_norm
    d_attn = (gate_one * d_middle).astype(BF16)
    d_gate_one = jnp.sum(d_middle * attn_out, axis=1)
    g_output_w = jnp.einsum("lsd,lse->de", attended, d_attn, preferred_element_type=F32)
    g_output_b = jnp.sum(d_attn.astype(F32), axis=(0, 1))
    d_attended = jnp.einsum("lse,de->lsd", d_attn, w_output, preferred_element_type=F32)
    d_attended = d_attended.astype(BF16).reshape(latents, seq_len, HEADS, HEAD_DIM)
    d_probs = jnp.einsum("lqhd,lkhd->lhqk", d_attended, value_heads, preferred_element_type=F32)
    delta_sum = jnp.sum(probs * d_probs, axis=-1, keepdims=True)
    d_scores = (probs * (d_probs - delta_sum)).astype(BF16)
    d_values = jnp.einsum("lhqk,lqhd->lkhd", probs_low, d_attended, preferred_element_type=F32)
    d_queries = (
        jnp.einsum("lhqk,lkhd->lqhd", d_scores, key_heads, preferred_element_type=F32) * score_scale
    )
    d_keys = (
        jnp.einsum("lhqk,lqhd->lkhd", d_scores, query_heads, preferred_element_type=F32) * score_scale
    )
    d_projected = jnp.concatenate(
        [t.reshape(latents, seq_len, D) for t in (d_queries, d_keys, d_values)], axis=-1
    ).astype(BF16)
    g_attend_w = jnp.einsum("lsd,lse->de", normed_one, d_projected, preferred_element_type=F32)
    column_sums = jnp.sum(d_projected.astype(F32), axis=(0, 1))
    g_query_value = jnp.concatenate([column_sums[:D], column_sums[2 * D :]])
    d_norm_one = jnp.einsum("lse,de->lsd", d_projected, w_attend, preferred_element_type=F32)
    _, norm_back = jax.vjp(modulate_norm, tokens_float, shift_one, scale_one)
    d_in_norm, d_shift_one, d_scale_one = norm_back(d_norm_one)
    grad_work = d_middle + d_in_norm
    d_modulation = jnp.concatenate(
        [
            d_shift_one[:, 0],
            d_scale_one[:, 0],
            d_gate_one,
            d_shift_two[:, 0],
            d_scale_two[:, 0],
            d_gate_two,
        ],
        axis=-1,
    ).astype(BF16)
    return finish(
        rank, replicas, latents, local_len, cond_float, cond_act_all, modulate_weight, tokens_out,
        grad_work, d_modulation, g_attend_w, g_query_value, g_output_w, g_output_b, g_expand_w,
        g_expand_b, g_shrink_w, g_shrink_b,
    )


def finish(
    rank, replicas, latents, local_len, cond_float, cond_act_all, modulate_weight, tokens_out,
    grad_work, d_modulation, g_attend_w, g_query_value, g_output_w, g_output_b, g_expand_w,
    g_expand_b, g_shrink_w, g_shrink_b,
):
    def in_order(own, other):
        return jnp.where(rank == 0, jnp.concatenate([own, other]), jnp.concatenate([other, own]))

    def give_back(values):
        own = lax.dynamic_slice_in_dim(values, rank * local_len, local_len, 1)
        away = lax.dynamic_slice_in_dim(values, (1 - rank) * local_len, local_len, 1)
        other = lax.ppermute(away.astype(BF16), "shard", SWAP).astype(values.dtype)
        return in_order(own, other)

    grads = jnp.concatenate(
        [in_halves(g.astype(BF16)) for g in (g_shrink_w, g_expand_w, g_attend_w, g_output_w)], axis=1
    )
    own_cond = lax.dynamic_slice_in_dim(cond_act_all, rank * latents, latents, 0)
    bias_all = jnp.concatenate([g_query_value, g_output_b, g_expand_b, g_shrink_b]).astype(BF16)
    flat = jnp.concatenate([d_modulation.reshape(-1), own_cond.reshape(-1), bias_all])
    block = jnp.pad(flat, (0, BLOCK_ROWS * 128 - flat.shape[0])).reshape(BLOCK_ROWS, 128)
    tokens_result = give_back(tokens_out)
    grad_result = give_back(grad_work)
    d_mod_other = lax.ppermute(d_modulation, "shard", SWAP)
    d_cond_part = jnp.einsum(
        "le,de->ld", in_order(d_modulation, d_mod_other), modulate_weight, preferred_element_type=F32
    )
    d_cond_other = lax.ppermute(d_cond_part, "shard", SWAP)
    d_cond = jnp.where(
        rank == 0,
        jnp.concatenate([d_cond_part, d_cond_other], axis=1),
        jnp.concatenate([d_cond_other, d_cond_part], axis=1),
    )
    _, silu_back = jax.vjp(jax.nn.silu, cond_float)
    grad_condition = silu_back(d_cond)[0]

    reduced, blocks = reduce_all(grads, block, replicas)
    flat_blocks = blocks.reshape(2 * replicas, BLOCK_ROWS * 128)
    n_mod, n_cond = latents * 6 * D, latents * D
    d_mod_all = flat_blocks[:, :n_mod].reshape(-1, 6 * D)
    act_all = flat_blocks[:, n_mod : n_mod + n_cond].reshape(-1, D)
    bias_sum = jnp.sum(flat_blocks[:, n_mod + n_cond : n_mod + n_cond + bias_all.shape[0]].astype(F32), axis=0)
    own_act = lax.dynamic_slice_in_dim(act_all, rank * (D // 2), D // 2, 1)
    g_modulate_w = jnp.einsum("lr,le->re", own_act, d_mod_all, preferred_element_type=F32)
    g_modulate_b = jnp.sum(
        lax.dynamic_slice_in_dim(d_mod_all, rank * 3 * D, 3 * D, 1).astype(F32), axis=0
    )

    def own_bias(start, size):
        return lax.dynamic_slice_in_dim(bias_sum, start + rank * (size // 2), size // 2, 0)

    reduced = reduced.astype(F32)
    half = D // 2
    expand = jnp.concatenate([reduced[768 + i * half : 768 + (i + 1) * half] for i in range(4)], axis=1)
    attend = jnp.concatenate([reduced[1536 + i * half : 1536 + (i + 1) * half] for i in range(3)], axis=1)
    return (
        tokens_result,
        grad_result,
        grad_condition,
        g_modulate_w,
        g_modulate_b,
        attend,
        own_bias(0, 2 * D),
        reduced[1536 + 3 * half :],
        own_bias(2 * D, D),
        expand,
        own_bias(3 * D, FF),
        reduced[:768],
        own_bias(3 * D + FF, D),
    )


def solution(mesh):
    specs = (
        P("shard", None),
        P("shard"),
        P("shard", None),
        P("shard"),
        P("shard", None),
        P("shard"),
        P("shard", None),
        P("shard"),
        P("shard", None),
        P("shard"),
    )
    tokens = P("replica", "shard", None)
    return jax.shard_map(
        on_device,
        mesh=mesh,
        in_specs=(tokens, P("replica", None), tokens) + specs,
        out_specs=(tokens, tokens, P("replica", None)) + specs,
        check_vma=False,
    )
```

time: 453 us -> 230 us (0.51)
  waiting for transfers between devices: 205 us -> 1.54 us
  blocking collectives: 140 us -> 0 us
  Pallas kernels: 0 us -> 125 us
  between operations: 17.7 us -> 1.24 us
  local copies, waits for them, and re-layouts: 28.7 us -> 42.2 us
  matrix products: 47 us -> 36.2 us
    reduce_scatter x6 -> x0, waiting for transfers between devices: 141 us -> none  [the longest x1 37.1 us: on_device(): lax.psum_scatter(widening_weight_gradient, 'shard', scatter_dimension=0,...]
    pallas_call x0 -> x2, Pallas kernels: none -> 125 us  [the longest x1 70 us: gather_all(): pl.pallas_call(gather_kernel, out_shape=(tokens, tokens, jax.ShapeDtypeSt...]
    psum x2 -> x0, blocking collectives: 72.2 us -> none  [the longest x1 63.6 us: on_device(): lax.psum((g_modulate_w, g_modulate_b, owned[0], owned[1], owned[2], owned...]
    psum x1 -> x0, waiting for transfers between devices: 62.1 us -> none  [on_device(): lax.psum((g_modulate_w, g_modulate_b, owned[0], owned[1], owned[2], owned...]
    all_gather x7 -> x0, blocking collectives: 61.7 us -> none  [the longest x1 14.9 us: on_device(): lax.all_gather(values_local, 'shard', axis=1, tiled=True)]
    slice x2 -> x19, local copies, waits for them, and re-layouts: 1.12 us -> 8.24 us  [the longest x2 2.82 us: in_halves(): gradient[:, i:i + D].reshape(2, rows, D)]
    dynamic_slice x1 -> x7, local copies, waits for them, and re-layouts: 0.08 us -> 6.24 us  [the longest x3 4.09 us: own_bias(): lax.dynamic_slice_in_dim(bias_sum, start + rank * (size // 2), size // 2, 0)]
    unnamed x1 -> x0, blocking collectives: 5.82 us -> none
  transfers between devices with their start and end apart: 10 -> 4, of which waited for: 7 -> 1; matrix products, arithmetic and copies ran while one was open for 13% -> 18% of each run, Pallas kernels for 0% -> 24%
where the time goes in v1:
time: 230 us; the launch traced here: 229 us
  Pallas kernels  125 us (54%)
  local copies, waits for them, and re-layouts  42.2 us (18%)
  matrix products  36.2 us (16%)
  other arithmetic  17.5 us (8%)
  starting transfers between devices  5.1 us (2%)
    pallas_call x1, Pallas kernels, gather_all(): pl.pallas_call(gather_kernel, out_shape=(tokens, tokens, jax.ShapeDtypeSt...  70 us
    pallas_call x1, Pallas kernels, reduce_all(): pl.pallas_call(functools.partial(reduce_kernel, bits), out_shape=(jax.Sha...  54.9 us
    unnamed x92, local copies, waits for them, and re-layouts  13.7 us
    reshape x3, local copies, waits for them, and re-layouts, on_device(): t.reshape(latents, seq_len, D)  4.74 us
  transfers between devices with their start and end apart: 4, of which 1 were waited for; matrix products, arithmetic and copies ran while one was open for 18% of the time, Pallas kernels for 24%

profile of v1, /device:TPU:0, one launch (start us, length us, event | category | flops | bytes accessed | tf_op | source)
XLA Modules:
  0.0 228.7 jit_solution(3376408814498624703)
XLA Ops:
  0.7 3.6 %concatenate.119 = bf16[2688]{0:T(1024)(128)(2,1)S(1)} concatenate(bf16[1152]{0:T(1024)(128)(2,1)} %param.17, bf16[384]{0:T(512)(128)(2,1)} %param.19, bf16[192]{0:T(256)(128)(2,1)} %param.21, bf16[768]{0:T(1024)(128)(2,1)} %param.23, bf16[192]{0:T(256)(128)(2,1)} %param.25), dimensions={0} | concatenate | bytes 10752 | tf_op jit(solution)/shard_map/concatenate | solution.py:344
  5.9 70.0 %shard_map.228 = (bf16[2,256,384]{2,1,0:T(8,128)(2,1)}, bf16[2,256,384]{2,1,0:T(8,128)(2,1)}, f32[64,128]{1,0:T(8,128)}, bf16[384,1152]{1,0:T(8,128)(2,1)}, bf16...) custom-call(bf16[4,128,384]{2,1,0:T(8,128)(2,1)} %tok.1, bf16[4,128,384]{2,1,0:T(8,128)(2,1)} %cot.1, ...), custom_call_target="tpu_custom_call" | custom-call | tf_op jit(solution)/shard_map/pallas_call | solution.py:149
  79.2 1.1 convert_reduce_fusion
  80.3 1.3 fusion.32
  81.6 2.2 fusion.7
  86.9 1.3 fusion.72
  88.6 1.0 convolution_add_fusion.1
  89.7 3.6 %fusion.83 = (bf16[1536]{0:T(1024)(128)(2,1)}, bf16[2,256,1536]{2,1,0:T(8,128)(2,1)S(1)}) fusion(f32[2,256,1536]{2,1,0:T(8,128)S(1)} %convolution_add_fusion.1, bf16[1536,384]{1,0:T(8,128)(2,1)S(1)} %copy-done.30, bf16[2,256,384]{2,1,0:T(8,128)(2,1)S(1)} %copy-done.21, f32[2,384]{1,0:T(2,128)S(1)} %get-tuple-element.68), kind=kOutput, calls=%fused_computation.174 | convolution fusion | flops 621083136 | bytes 6297600 | tf_op jit(solution)/shard_map/het,jt->hej/dot_general | solution.py:416
  93.3 1.1 multiply_reduce_fusion.2
  94.8 0.9 copy-done.10
  95.7 0.8 fusion.70
  96.5 1.2 convolution_convert_fusion.2
  97.7 1.9 copy.50
  99.6 3.6 %convolution_convert_fusion = bf16[2,6,64,256]{3,2,1,0:T(8,128)(2,1)} fusion(bf16[2,256,6,64]{1,3,2,0:T(8,128)(2,1)} %bitcast.111, f32[2,6,256,256]{2,3,1,0:T(8,128)} %copy-done.2, f32[2,6,256]{2,1,0:T(8,128)S(1)} %log_add_fusion), kind=kOutput, calls=%fused_computation.30 | convolution fusion | flops 103219200 | bytes 3944448 | tf_op jit(solution)/shard_map/lhqk,lqhd->lkhd/dot_general | solution.py:434
  103.2 0.9 multiply_reduce_fusion
  104.9 1.3 fusion.13
  106.2 1.1 fusion.12
  107.3 1.9 copy.56
  109.3 0.9 copy.55
  110.2 1.9 copy.54
  112.1 2.5 %fusion.33 = (f32[2,256]{1,0:T(2,128)S(1)}, f32[2,256,384]{2,1,0:T(8,128)S(1)}) fusion(bf16[2,256,384]{2,1,0:T(8,128)(2,1)S(1)} %copy-done.4, f32[2,384]{1,0:T(2,128)S(1)} %get-tuple-element.72, f32[2,256]{1,0:T(2,128)S(1)} %broadcast_multiply_fusion.1, bf16[384,1152]{1,0:T(8,128)(2,1)} %get-tuple-element.24, bf16[2,256,384]{2,1,0:T(8,128)(2,1)} %copy.56, ...), kind=kOutput, calls=%fused_computation.65 | convolution fusion | flops 457506304 | bytes 3251200 | tf_op jit(solution)/shard_map/lse,de->lsd/dot_general | solution.py:447
  114.6 0.9 copy-done.19
  116.0 4.6 %fusion.35 = (bf16[2,384]{1,0:T(2,128)(2,1)S(1)}, bf16[2,384]{1,0:T(2,128)(2,1)S(1)}, f32[2,256,384]{2,1,0:T(8,128)S(1)}, bf16[2,256,384]{2,1,0:T(8,128)(2,1)S(1)}) fusion(bf16[2,256,384]{2,1,0:T(8,128)(2,1)} %get-tuple-element.28, f32[2,256,384]{2,1,0:T(8,128)} %get-tuple-element.86, f32[2,256,384]{2,1,0:T(8,128)S(1)} %copy-done.11, ...), kind=kOutput, calls=%fused_computation.67 | convolution fusion | flops 614988288 | bytes 9458176 | tf_op jit(solution)/shard_map/ega,ap->egp/dot_general | solution.py:407
  120.6 0.8 constant_dynamic-slice_fusion.3
  121.4 1.5 collective-permute-start
  124.2 1.5 collective-permute-start.2
  126.5 2.5 %fusion.8 = bf16[1536,384]{1,0:T(8,128)(2,1)} fusion(bf16[2,256,384]{2,1,0:T(8,128)(2,1)S(1)} %copy-done.22, f32[2,384]{1,0:T(2,128)S(1)} %get-tuple-element.68, f32[2,256,1536]{2,1,0:T(8,128)S(1)} %copy-done.33), kind=kOutput, calls=%fused_computation.20 | convolution fusion | flops 612237312 | bytes 4721664 | tf_op jit(solution)/shard_map/ukq,ukc->qc/dot_general | solution.py:414
  129.1 2.0 fusion.9
  131.0 1.8 fusion.10
  134.7 2.4 %constant_dynamic-update-slice_fusion.14 = bf16[2,2304,384]{2,1,0:T(8,128)(2,1)} fusion(bf16[2,768,384]{2,1,0:T(8,128)(2,1)} %bitcast.128), kind=kLoop, calls=%fused_computation.105 | loop fusion | bytes 2359296
  137.1 1.4 fusion.74
  138.5 1.5 fusion.76
  147.7 2.0 copy-done.1
  149.7 54.9 %shard_map.229 = (bf16[2304,384]{1,0:T(8,128)(2,1)S(1)}, bf16[32,80,128]{2,1,0:T(8,128)(2,1)S(1)}) custom-call(bf16[2,2304,384]{2,1,0:T(8,128)(2,1)S(1)} %copy-done.1, bf16[80,128]{1,0:T(8,128)(2,1)S(1)} %pad_bitcast_fusion.block), custom_call_target="tpu_custom_call" | custom-call | tf_op jit(solution)/shard_map/pallas_call | solution.py:281
  206.3 1.2 fusion.73
  207.5 2.5 %fusion.47 = f32[192,2304]{1,0:T(8,128)} fusion(bf16[64,2304]{1,0:T(8,128)(2,1)S(1)} %reshape.320, bf16[64,384]{1,0:T(8,128)(2,1)} %reshape.319, s32[]{:T(128)S(6)} %select_n.117), kind=kOutput, calls=%fused_computation.89 | convolution fusion | flops 56623104 | bytes 2097156 | tf_op jit(solution)/shard_map/lr,le->re/dot_general | solution.py:512
  210.0 1.9 pad_maximum_fusion.2
  211.9 2.4 %pad_maximum_fusion.1 = f32[192,1536]{1,0:T(8,128)} fusion(f32[192,384]{1,0:T(8,128)} %get-tuple-element.48, f32[192,384]{1,0:T(8,128)} %get-tuple-element.47, f32[192,384]{1,0:T(8,128)} %get-tuple-element.46, f32[192,384]{1,0:T(8,128)} %get-tuple-element.45), kind=kLoop, calls=%fused_computation.49 | loop fusion | flops 884736 | bytes 2359296 | tf_op jit(solution)/shard_map/concatenate | solution.py:522
  214.3 1.4 fusion.78
  215.7 1.1 slice.227
  216.8 1.3 dynamic_slice.52
  218.2 1.4 dynamic_slice.54
  219.5 1.1 fusion.49
  220.6 1.5 collective-permute-start.3
  222.7 1.5 collective-permute-done.3
  225.0 1.0 convert_element_type.129
  225.9 0.9 maximum_select_fusion
  226.9 1.8 maximum_select_fusion.1
  (158 shorter events, 24.5 us)
Async XLA Ops:
  0.6 4.3 %copy-start = (bf16[192,2304]{1,0:T(8,128)(2,1)S(1)}, bf16[192,2304]{1,0:T(8,128)(2,1)}, u32[]{:S(2)}) copy-start(bf16[192,2304]{1,0:T(8,128)(2,1)} %param.16) | copy-start | bytes 2654212
  84.1 1.6 copy-start.5
  85.2 1.7 copy-start.2
  85.2 1.8 copy-start.4
  85.2 1.8 copy-start.18
  85.8 2.8 %copy-start.31 = (bf16[384,1536]{1,0:T(8,128)(2,1)S(1)}, bf16[384,1536]{1,0:T(8,128)(2,1)}, u32[]{:S(2)}) copy-start(bf16[384,1536]{1,0:T(8,128)(2,1)} %get-tuple-element.26) | copy-start | bytes 3538948
  86.9 2.8 %copy-start.8 = (bf16[2,6,64,256]{3,2,1,0:T(8,128)(2,1)}, bf16[2,6,64,256]{3,2,1,0:T(8,128)(2,1)S(1)}, u32[]{:S(2)}) copy-start(bf16[2,6,64,256]{3,2,1,0:T(8,128)(2,1)S(1)} %convolution_convert_fusion.1) | copy-start | bytes 1179652
  88.3 1.4 copy-start.21
  88.3 1.4 copy-start.30
  89.6 3.6 %copy-start.32 = (f32[2,256,1536]{2,1,0:T(8,128)}, f32[2,256,1536]{2,1,0:T(8,128)S(1)}, u32[]{:S(2)}) copy-start(f32[2,256,1536]{2,1,0:T(8,128)S(1)} %convolution_add_fusion.1) | copy-start | bytes 9437188
  93.3 1.6 copy-start.34
  94.8 0.9 copy-start.10
  99.6 3.6 %copy-start.3 = (f32[2,6,256,256]{2,3,1,0:T(8,128)S(1)}, f32[2,6,256,256]{2,3,1,0:T(8,128)}, u32[]{:S(2)}) copy-start(f32[2,6,256,256]{2,3,1,0:T(8,128)} %copy-done.2) | copy-start | bytes 9437188
  99.6 3.6 %copy-start.6 = (bf16[2,256,384]{1,2,0:T(8,128)(2,1)S(1)}, bf16[2,256,384]{1,2,0:T(8,128)(2,1)}, u32[]{:S(2)}) copy-start(bf16[2,256,384]{1,2,0:T(8,128)(2,1)} %copy-done.5) | copy-start | bytes 1179652
  99.6 3.6 %copy-start.7 = (bf16[2,256,384]{1,2,0:T(8,128)(2,1)S(1)}, bf16[2,256,384]{1,2,0:T(8,128)(2,1)}, u32[]{:S(2)}) copy-start(bf16[2,256,384]{1,2,0:T(8,128)(2,1)} %copy.50) | copy-start | bytes 1179652
  106.2 3.1 %copy-start.12 = (bf16[2,6,64,256]{3,2,1,0:T(8,128)(2,1)S(1)}, bf16[2,6,64,256]{3,2,1,0:T(8,128)(2,1)}, u32[]{:S(2)}) copy-start(bf16[2,6,64,256]{3,2,1,0:T(8,128)(2,1)} %fusion.13) | copy-start | bytes 1179652
  112.1 3.9 %copy-start.11 = (f32[2,256,384]{2,1,0:T(8,128)S(1)}, f32[2,256,384]{2,1,0:T(8,128)}, u32[]{:S(2)}) copy-start(f32[2,256,384]{2,1,0:T(8,128)} %copy-done.10) | copy-start | bytes 2359300
  114.6 0.9 copy-start.19
  116.0 10.5 %copy-start.22 = (bf16[2,256,384]{2,1,0:T(8,128)(2,1)S(1)}, bf16[2,256,384]{2,1,0:T(8,128)(2,1)}, u32[]{:S(2)}) copy-start(bf16[2,256,384]{2,1,0:T(8,128)(2,1)} %get-tuple-element.28) | copy-start | bytes 1179652
  116.0 10.5 %copy-start.33 = (f32[2,256,1536]{2,1,0:T(8,128)S(1)}, f32[2,256,1536]{2,1,0:T(8,128)}, u32[]{:S(2)}) copy-start(f32[2,256,1536]{2,1,0:T(8,128)} %copy-done.32) | copy-start | bytes 9437188
  121.4 105.4 %collective-permute-start = (bf16[2,128,384]{2,1,0:T(8,128)(2,1)}, bf16[2,128,384]{2,1,0:T(8,128)(2,1)}, u32[]{:S(2)}, u32[]{:S(2)}) collective-permute-start(bf16[2,128,384]{2,1,0:T(8,128)(2,1)} %get-tuple-element.67), channel_id=1, source_target_pairs={{0,1},{1,0},{2,3},{3,2},{4,5},{5,4},{6,7},{7,6},{8,9},{9,8},{10,11... | collective-permute-start | bytes 589832 | tf_op jit(solution)/shard_map/ppermute | solution.py:480
  123.6 101.3 %collective-permute-start.1 = (bf16[2,128,384]{2,1,0:T(8,128)(2,1)}, bf16[2,128,384]{2,1,0:T(8,128)(2,1)}, u32[]{:S(2)}, u32[]{:S(2)}) collective-permute-start(bf16[2,128,384]{2,1,0:T(8,128)(2,1)} %dynamic-slice_convert_fusion), channel_id=1, source_target_pairs={{0,1},{1,0},{2,3},{3,2},{4,5},{5,4},{6,7},{7,6},{8,9},{9,8},{10,11... | collective-permute-start | bytes 589832 | tf_op jit(solution)/shard_map/ppermute | solution.py:480
  124.2 95.3 %collective-permute-start.2 = (bf16[2,2304]{1,0:T(2,128)(2,1)S(1)}, bf16[2,2304]{1,0:T(2,128)(2,1)}, u32[]{:S(2)}, u32[]{:S(2)}) collective-permute-start(bf16[2,2304]{1,0:T(2,128)(2,1)S(1)} %constant_dynamic-update-slice_fusion), channel_id=1, source_target_pairs={{0,1},{1,0},{2,3},{3,2},{4,5},{5,4},{6,7},{7,6},{8,9},{9,8},{10,11... | collective-permute-start | bytes 27656 | tf_op jit(solution)/shard_map/ppermute | solution.py:492
  126.5 2.5 %copy-start.35 = (bf16[2,256,1536]{2,1,0:T(8,128)(2,1)S(1)}, bf16[2,256,1536]{2,1,0:T(8,128)(2,1)}, u32[]{:S(2)}) copy-start(bf16[2,256,1536]{2,1,0:T(8,128)(2,1)} %copy-done.34) | copy-start | bytes 4718596
  129.1 2.0 copy-start.13
  129.1 2.0 copy-start.14
  129.1 2.0 copy-start.15
  131.0 1.8 copy-start.9
  131.0 3.4 %copy-start.16 = (bf16[2,256,384]{2,1,0:T(8,128)(2,1)S(1)}, bf16[2,256,384]{2,1,0:T(8,128)(2,1)}, u32[]{:S(2)}) copy-start(bf16[2,256,384]{2,1,0:T(8,128)(2,1)} %copy.54) | copy-start | bytes 1179652
  134.6 5.3 %copy-start.26 = (bf16[2,384]{1,0:T(2,128)(2,1)S(1)}, bf16[2,384]{1,0:T(2,128)(2,1)}, u32[]{:S(2)}) copy-start(bf16[2,384]{1,0:T(2,128)(2,1)} %constant_dynamic-slice_fusion) | copy-start | bytes 4612
  134.6 5.4 %copy-start.23 = (bf16[4608]{0:T(1024)(128)(2,1)S(1)}, bf16[4608]{0:T(1024)(128)(2,1)}, u32[]{:S(2)}) copy-start(bf16[4608]{0:T(1024)(128)(2,1)} %convert_element_type.135) | copy-start | bytes 27652
  134.6 5.4 %copy-start.24 = (bf16[8448]{0:T(1024)(128)(2,1)S(1)}, bf16[8448]{0:T(1024)(128)(2,1)}, u32[]{:S(2)}) copy-start(bf16[8448]{0:T(1024)(128)(2,1)} %custom-call) | copy-start | bytes 50692
  134.6 6.4 %copy-start.28 = (bf16[384]{0:T(512)(128)(2,1)S(1)}, bf16[384]{0:T(512)(128)(2,1)}, u32[]{:S(2)}) copy-start(bf16[384]{0:T(512)(128)(2,1)} %get-tuple-element.39) | copy-start | bytes 2308
  134.6 6.6 %copy-start.29 = (bf16[1536]{0:T(1024)(128)(2,1)S(1)}, bf16[1536]{0:T(1024)(128)(2,1)}, u32[]{:S(2)}) copy-start(bf16[1536]{0:T(1024)(128)(2,1)} %get-tuple-element.92) | copy-start | bytes 9220
  134.7 6.8 %copy-start.27 = (bf16[384]{0:T(512)(128)(2,1)S(1)}, bf16[384]{0:T(512)(128)(2,1)}, u32[]{:S(2)}) copy-start(bf16[384]{0:T(512)(128)(2,1)} %get-tuple-element.65) | copy-start | bytes 2308
  147.7 2.0 copy-start.1
  211.9 12.4 %copy-start.25 = (bf16[4,384]{1,0:T(4,128)(2,1)S(1)}, bf16[4,384]{1,0:T(4,128)(2,1)}, u32[]{:S(2)}) copy-start(bf16[4,384]{1,0:T(4,128)(2,1)} %param.14) | copy-start | bytes 9220
  211.9 14.0 %copy-start.17 = (f32[2,128,384]{2,1,0:T(8,128)S(1)}, f32[2,128,384]{2,1,0:T(8,128)}, u32[]{:S(2)}) copy-start(f32[2,128,384]{2,1,0:T(8,128)} %constant_dynamic-slice_fusion.1) | copy-start | bytes 1179652
  214.3 12.5 %copy-start.20 = (bf16[2,128,384]{2,1,0:T(8,128)(2,1)S(1)}, bf16[2,128,384]{2,1,0:T(8,128)(2,1)}, u32[]{:S(2)}) copy-start(bf16[2,128,384]{2,1,0:T(8,128)(2,1)} %get-tuple-element.66) | copy-start | bytes 589828
  220.6 3.7 %collective-permute-start.3 = (f32[4,192]{1,0:T(4,128)S(1)}, f32[4,192]{1,0:T(4,128)S(1)}, u32[]{:S(2)}, u32[]{:S(2)}) collective-permute-start(f32[4,192]{1,0:T(4,128)S(1)} %fusion.49), channel_id=1, source_target_pairs={{0,1},{1,0},{2,3},{3,2},{4,5},{5,4},{6,7},{7,6},{8,9},{9,8},{10,11... | collective-permute-start | bytes 9224 | tf_op jit(solution)/shard_map/ppermute | solution.py:496

commit v2 on v1

--- a/solution.py
+++ b/solution.py
@@ -18,17 +18,6 @@
 SWAP = [(0, 1), (1, 0)]
 
 
-def modulate_norm(values, shift, scale):
-    average = jnp.mean(values, axis=-1, keepdims=True)
-    centered = values - average
-    variance = jnp.mean(centered * centered, axis=-1, keepdims=True)
-    return centered * lax.rsqrt(variance + 1e-06) * (1.0 + scale) + shift
-
-
-def gelu_tanh(values):
-    return jax.nn.gelu(values, approximate=True)
-
-
 def flip(index, bit):
     step = 1 << bit
     return index + step - 2 * step * ((index // step) % 2)
@@ -89,13 +78,14 @@
     first = []
     for k, (own, full) in enumerate(pairs):
         n = own.shape[0] // 4
-        c = remote(
-            own.at[pl.ds(pl.multiple_of(quarter * n, n), n)], rows_at(full, s, quarter),
-            send_w.at[k, 0], recv_w.at[k, 0], over_x,
-        )
-        c.start()
-        first.append(c)
-    swaps[2].start()
+        first.append(
+            remote(
+                own.at[pl.ds(pl.multiple_of(quarter * n, n), n)], rows_at(full, s, quarter),
+                send_w.at[k, 0], recv_w.at[k, 0], over_x,
+            )
+        )
+    first[0].start()
+    first[1].start()
     locals_ = []
     for k, (src, dst) in enumerate(((tok, tok_all), (cot, cot_all))):
         locals_.append(
@@ -109,14 +99,24 @@
     for c in locals_:
         c.start()
     later = []
-    for k, (own, full) in enumerate(pairs):
+
+    def forward(k):
         first[k].wait_recv()
-        mine = rows_at(full, o, quarter)
+        mine = rows_at(pairs[k][1], o, quarter)
         by_y = remote(mine, mine, send_w.at[k, 1], recv_w.at[k, 1], over_y)
         by_y.start()
         by_core = remote(mine, mine, send_w.at[k, 2], recv_w.at[k, 2], over_core)
         by_core.start()
         later.append((by_y, by_core))
+
+    swaps[1].wait_recv()
+    first[2].start()
+    forward(0)
+    forward(1)
+    first[3].start()
+    forward(2)
+    swaps[2].start()
+    forward(3)
     last = []
     for k, (own, full) in enumerate(pairs):
         later[k][0].wait_recv()
@@ -127,7 +127,7 @@
     for k in range(4):
         later[k][1].wait_recv()
         last[k].wait_recv()
-    for c in swaps:
+    for c in (swaps[0], swaps[2]):
         c.wait_recv()
     for c in locals_:
         c.wait()
@@ -307,10 +307,195 @@
     )(grads, block)
 
 
-def in_halves(gradient):
-    rows = gradient.shape[0] // 2
-    columns = [gradient[:, i : i + D].reshape(2, rows, D) for i in range(0, gradient.shape[1], D)]
-    return jnp.concatenate(columns, axis=1) if len(columns) > 1 else columns[0]
+def dot_nn(a, b):
+    return lax.dot_general(a, b, (((1,), (0,)), ((), ())), preferred_element_type=F32)
+
+
+def dot_nt(a, b):
+    return lax.dot_general(a, b, (((1,), (1,)), ((), ())), preferred_element_type=F32)
+
+
+def dot_tn(a, b):
+    return lax.dot_general(a, b, (((0,), (0,)), ((), ())), preferred_element_type=F32)
+
+
+def row_sum(values):
+    return jnp.sum(values, axis=0, keepdims=True)
+
+
+def normalise(values):
+    centered = values - jnp.mean(values, axis=-1, keepdims=True)
+    inverse = lax.rsqrt(jnp.mean(centered * centered, axis=-1, keepdims=True) + 1e-06)
+    return centered * inverse, inverse
+
+
+def normalise_back(grad, unit, inverse, scale):
+    grad = grad * (1.0 + scale)
+    inner = jnp.mean(grad * unit, axis=-1, keepdims=True)
+    return inverse * (grad - jnp.mean(grad, axis=-1, keepdims=True) - unit * inner)
+
+
+def block_kernel(
+    tok, cot, mod, b_attend, b_output, b_expand, b_shrink, wa, wo, ww, wn,
+    tok_out, grad_tok, d_mod, grads, b_grads,
+    n_one, proj, att, n_two, hidden, d_mlp_all, d_pre_all, d_attn_all, d_proj, probs,
+):
+    step = pl.program_id(0)
+    seq = tok.shape[1]
+    at = pl.ds(pl.multiple_of(step * seq, seq), seq)
+    shift_one, scale_one, gate_one, shift_two, scale_two, gate_two = (
+        mod[0, :, i * D : (i + 1) * D] for i in range(6)
+    )
+    lane = lax.broadcasted_iota(jnp.int32, (1, 2 * HEAD_DIM), 1)
+    masks = [
+        jnp.where(lane < HEAD_DIM, 1.0, 0.0).astype(BF16),
+        jnp.where(lane < HEAD_DIM, 0.0, 1.0).astype(BF16),
+    ]
+    width = 2 * HEAD_DIM
+    score_scale = HEAD_DIM ** (-0.5)
+
+    @pl.when(step == 0)
+    def _():
+        b_grads[...] = jnp.zeros_like(b_grads)
+
+    def add_bias(start, value):
+        b_grads[:, start : start + value.shape[1]] += row_sum(value.astype(F32))
+
+    x = tok[0].astype(F32)
+    unit_one, inv_one = normalise(x)
+    n_one[at] = (unit_one * (1.0 + scale_one) + shift_one).astype(BF16)
+    for i in range(3):
+        cols = slice(i * D, (i + 1) * D)
+        proj[:, cols] = (dot_nn(n_one[at], wa[:, cols]) + b_attend[:, cols]).astype(BF16)
+    for p in range(HEADS // 2):
+        cols = slice(p * width, (p + 1) * width)
+        query = proj[:, cols]
+        key = proj[:, D + p * width : D + (p + 1) * width]
+        value = proj[:, 2 * D + p * width : 2 * D + (p + 1) * width]
+        total = None
+        for h in range(2):
+            scores = dot_nt(query, key * masks[h]) * score_scale
+            expo = jnp.exp(scores - jnp.max(scores, axis=-1, keepdims=True))
+            prob = expo * (1.0 / jnp.sum(expo, axis=-1, keepdims=True))
+            probs[2 * p + h] = prob
+            part = dot_nn(prob.astype(BF16), value * masks[h])
+            total = part if total is None else total + part
+        att[at, cols] = total.astype(BF16)
+    attn_out = dot_nn(att[at], wo[...]) + b_output[...]
+    middle = x + gate_one * attn_out
+    unit_two, inv_two = normalise(middle)
+    n_two[at] = (unit_two * (1.0 + scale_two) + shift_two).astype(BF16)
+    up = cot[0].astype(F32)
+    d_mlp = (gate_two * up).astype(BF16)
+    d_mlp_all[at] = d_mlp
+    add_bias(3 * D + FF, d_mlp)
+    mlp = jnp.zeros((seq, D), F32)
+    d_two = jnp.zeros((seq, D), F32)
+    c0 = (2.0 / jnp.pi) ** 0.5
+    for i in range(FF // D):
+        cols = slice(i * D, (i + 1) * D)
+        pre = dot_nn(n_two[at], ww[:, cols]) + b_expand[:, cols]
+        square = pre * pre
+        tanh = jnp.tanh(c0 * pre * (1.0 + 0.044715 * square))
+        act = (0.5 * pre * (1.0 + tanh)).astype(BF16)
+        slope = 0.5 * (1.0 + tanh) + 0.5 * pre * (1.0 - tanh * tanh) * (
+            c0 * (1.0 + 3 * 0.044715 * square)
+        )
+        hidden[at, cols] = act
+        mlp += dot_nn(act, wn[cols, :])
+        d_pre = (dot_nt(d_mlp, wn[cols, :]) * slope).astype(BF16)
+        d_pre_all[at, cols] = d_pre
+        add_bias(3 * D + i * D, d_pre)
+        d_two += dot_nt(d_pre, ww[:, cols])
+    mlp += b_shrink[...]
+    tok_out[0] = (middle + gate_two * mlp).astype(BF16)
+    d_mod[0, :, 5 * D : 6 * D] = row_sum(up * mlp)
+    d_mod[0, :, 3 * D : 4 * D] = row_sum(d_two)
+    d_mod[0, :, 4 * D : 5 * D] = row_sum(d_two * unit_two)
+    d_middle = up + normalise_back(d_two, unit_two, inv_two, scale_two)
+    d_attn = (gate_one * d_middle).astype(BF16)
+    d_attn_all[at] = d_attn
+    add_bias(2 * D, d_attn)
+    d_mod[0, :, 2 * D : 3 * D] = row_sum(d_middle * attn_out)
+    d_att = dot_nt(d_attn, wo[...]).astype(BF16)
+    for p in range(HEADS // 2):
+        cols = slice(p * width, (p + 1) * width)
+        query = proj[:, cols]
+        key = proj[:, D + p * width : D + (p + 1) * width]
+        value = proj[:, 2 * D + p * width : 2 * D + (p + 1) * width]
+        grad = d_att[:, cols]
+        d_q = d_k = d_v = None
+        for h in range(2):
+            prob = probs[2 * p + h]
+            d_prob = dot_nt(grad, value * masks[h])
+            delta = jnp.sum(prob * d_prob, axis=-1, keepdims=True)
+            d_score = (prob * (d_prob - delta)).astype(BF16)
+            parts = (
+                dot_nn(d_score, key * masks[h]),
+                dot_tn(d_score, query * masks[h]),
+                dot_tn(prob.astype(BF16), grad * masks[h]),
+            )
+            d_q, d_k, d_v = parts if h == 0 else (d_q + parts[0], d_k + parts[1], d_v + parts[2])
+        d_proj[at, cols] = (d_q * score_scale).astype(BF16)
+        d_proj[at, D + p * width : D + (p + 1) * width] = (d_k * score_scale).astype(BF16)
+        d_proj[at, 2 * D + p * width : 2 * D + (p + 1) * width] = d_v.astype(BF16)
+    add_bias(0, d_proj[at, :D])
+    add_bias(D, d_proj[at, 2 * D :])
+    d_one = dot_nt(d_proj[at], wa[...])
+    d_mod[0, :, 0:D] = row_sum(d_one)
+    d_mod[0, :, D : 2 * D] = row_sum(d_one * unit_one)
+    grad_tok[0] = d_middle + normalise_back(d_one, unit_one, inv_one, scale_one)
+
+    @pl.when(step == pl.num_programs(0) - 1)
+    def _():
+        half = D // 2
+        for i in range(4):
+            cols = slice(i * D, (i + 1) * D)
+            part = dot_tn(hidden[:, cols], d_mlp_all[...]).astype(BF16)
+            grads[i // 2, (i % 2) * D : (i % 2 + 1) * D] = part
+            part = dot_tn(n_two[...], d_pre_all[:, cols]).astype(BF16)
+            for h in range(2):
+                grads[h, 2 * D + i * half : 2 * D + (i + 1) * half] = part[h * half : (h + 1) * half]
+        for i in range(3):
+            part = dot_tn(n_one[...], d_proj[:, i * D : (i + 1) * D]).astype(BF16)
+            for h in range(2):
+                grads[h, 4 * D + i * half : 4 * D + (i + 1) * half] = part[h * half : (h + 1) * half]
+        part = dot_tn(att[...], d_attn_all[...]).astype(BF16)
+        for h in range(2):
+            grads[h, 4 * D + 3 * half : 4 * D + 4 * half] = part[h * half : (h + 1) * half]
+
+
+def block_all(tok, cot, mod, biases, weights):
+    latents, seq, _ = tok.shape
+    rows = latents * seq
+    each = pl.BlockSpec((1, seq, D), lambda i: (i, 0, 0))
+    mods = pl.BlockSpec((1, 1, 6 * D), lambda i: (i, 0, 0))
+
+    def whole(shape):
+        zeros = (0,) * len(shape)
+        return pl.BlockSpec(shape, lambda i: zeros)
+
+    scratch = [(rows, D), (seq, 3 * D), (rows, D), (rows, D), (rows, FF), (rows, D), (rows, FF), (rows, D), (rows, 3 * D)]
+    shared = list(biases) + list(weights)
+    flops = 2 * 3 * rows * (D * 3 * D + D * D + 2 * D * FF)
+    return pl.pallas_call(
+        block_kernel,
+        grid=(latents,),
+        out_shape=(
+            jax.ShapeDtypeStruct(tok.shape, BF16),
+            jax.ShapeDtypeStruct(tok.shape, F32),
+            jax.ShapeDtypeStruct((latents, 1, 6 * D), F32),
+            jax.ShapeDtypeStruct((2, CHUNKS * ROWS, D), BF16),
+            jax.ShapeDtypeStruct((1, 4 * D + FF), F32),
+        ),
+        in_specs=[each, each, mods] + [whole(w.shape) for w in shared],
+        out_specs=(each, each, mods, whole((2, CHUNKS * ROWS, D)), whole((1, 4 * D + FF))),
+        scratch_shapes=[pltpu.VMEM(n, BF16) for n in scratch] + [pltpu.VMEM((HEADS, seq, seq), F32)],
+        compiler_params=pltpu.CompilerParams(
+            vmem_limit_bytes=56 * 2**20, dimension_semantics=("arbitrary",)
+        ),
+        cost_estimate=pl.CostEstimate(flops=flops, bytes_accessed=12 * 2**20, transcendentals=rows * FF),
+    )(tok, cot, mod, *shared)
 
 
 def on_device(
@@ -330,10 +515,8 @@
 ):
     rank = lax.axis_index("shard")
     replicas = lax.axis_size("replica")
-    score_scale = HEAD_DIM ** (-0.5)
     latents = tokens_in.shape[0] // 2
     local_len = tokens_in.shape[1]
-    seq_len = 2 * local_len
     own_rows = D // 2
     cond_float = condition.astype(F32)
     cond_act_all = jax.nn.silu(cond_float).astype(BF16)
@@ -369,107 +552,24 @@
     b_expand = both(4 * D + D // 2, FF // 2)
     b_shrink = both(4 * D + D // 2 + FF // 2, D // 2)
 
-    tokens_float = tokens_in.astype(F32)
     modulation = mod_keep + mod_other + b_modulate
-    shift_one = modulation[:, None, 0:D]
-    scale_one = modulation[:, None, D : 2 * D]
-    gate_one = modulation[:, None, 2 * D : 3 * D]
-    shift_two = modulation[:, None, 3 * D : 4 * D]
-    scale_two = modulation[:, None, 4 * D : 5 * D]
-    gate_two = modulation[:, None, 5 * D : 6 * D]
-    normed_one = modulate_norm(tokens_float, shift_one, scale_one).astype(BF16)
     full_bias = jnp.concatenate([b_query_value[:D], jnp.zeros((D,), F32), b_query_value[D:]])
-    projected = (
-        jnp.einsum("lsd,de->lse", normed_one, w_attend, preferred_element_type=F32) + full_bias
-    ).astype(BF16)
-    query_heads = projected[..., :D].reshape(latents, seq_len, HEADS, HEAD_DIM)
-    key_heads = projected[..., D : 2 * D].reshape(latents, seq_len, HEADS, HEAD_DIM)
-    value_heads = projected[..., 2 * D :].reshape(latents, seq_len, HEADS, HEAD_DIM)
-    scores = (
-        jnp.einsum("lqhd,lkhd->lhqk", query_heads, key_heads, preferred_element_type=F32)
-        * score_scale
-    )
-    highest = jnp.max(scores, axis=-1, keepdims=True)
-    log_norm = highest + jnp.log(jnp.sum(jnp.exp(scores - highest), axis=-1, keepdims=True))
-    probs = jnp.exp(scores - log_norm)
-    probs_low = probs.astype(BF16)
-    attended = jnp.einsum("lhqk,lkhd->lqhd", probs_low, value_heads, preferred_element_type=F32)
-    attended = attended.reshape(latents, seq_len, D).astype(BF16)
-    attn_out = jnp.einsum("lsd,de->lse", attended, w_output, preferred_element_type=F32) + b_output
-    middle = tokens_float + gate_one * attn_out
-    second_normalized = modulate_norm(middle, shift_two, scale_two).astype(BF16)
-    hidden_pre = (
-        jnp.einsum("bei,ig->beg", second_normalized, widening_matrix, preferred_element_type=F32)
-        + b_expand
-    )
-    hidden_act = gelu_tanh(hidden_pre).astype(BF16)
-    mlp_out = (
-        jnp.einsum("ega,ap->egp", hidden_act, narrowing_matrix, preferred_element_type=F32) + b_shrink
-    )
-    tokens_out = (middle + gate_two * mlp_out).astype(BF16)
-
-    upstream = cotangent.astype(F32)
-    d_mlp = (gate_two * upstream).astype(BF16)
-    d_gate_two = jnp.sum(upstream * mlp_out, axis=1)
-    g_shrink_w = jnp.einsum("ukq,ukc->qc", hidden_act, d_mlp, preferred_element_type=F32)
-    g_shrink_b = jnp.sum(d_mlp.astype(F32), axis=(0, 1))
-    d_act = jnp.einsum("het,jt->hej", d_mlp, narrowing_matrix, preferred_element_type=F32)
-    _, gelu_back = jax.vjp(gelu_tanh, hidden_pre)
-    d_pre = gelu_back(d_act)[0].astype(BF16)
-    g_expand_w = jnp.einsum("mqo,mqz->oz", second_normalized, d_pre, preferred_element_type=F32)
-    g_expand_b = jnp.sum(d_pre.astype(F32), axis=(0, 1))
-    d_second = jnp.einsum("pkc,ac->pka", d_pre, widening_matrix, preferred_element_type=F32)
-    _, norm_back = jax.vjp(modulate_norm, middle, shift_two, scale_two)
-    d_mid_norm, d_shift_two, d_scale_two = norm_back(d_second)
-    d_middle = upstream + d_mid_norm
-    d_attn = (gate_one * d_middle).astype(BF16)
-    d_gate_one = jnp.sum(d_middle * attn_out, axis=1)
-    g_output_w = jnp.einsum("lsd,lse->de", attended, d_attn, preferred_element_type=F32)
-    g_output_b = jnp.sum(d_attn.astype(F32), axis=(0, 1))
-    d_attended = jnp.einsum("lse,de->lsd", d_attn, w_output, preferred_element_type=F32)
-    d_attended = d_attended.astype(BF16).reshape(latents, seq_len, HEADS, HEAD_DIM)
-    d_probs = jnp.einsum("lqhd,lkhd->lhqk", d_attended, value_heads, preferred_element_type=F32)
-    delta_sum = jnp.sum(probs * d_probs, axis=-1, keepdims=True)
-    d_scores = (probs * (d_probs - delta_sum)).astype(BF16)
-    d_values = jnp.einsum("lhqk,lqhd->lkhd", probs_low, d_attended, preferred_element_type=F32)
-    d_queries = (
-        jnp.einsum("lhqk,lkhd->lqhd", d_scores, key_heads, preferred_element_type=F32) * score_scale
-    )
-    d_keys = (
-        jnp.einsum("lhqk,lqhd->lkhd", d_scores, query_heads, preferred_element_type=F32) * score_scale
-    )
-    d_projected = jnp.concatenate(
-        [t.reshape(latents, seq_len, D) for t in (d_queries, d_keys, d_values)], axis=-1
-    ).astype(BF16)
-    g_attend_w = jnp.einsum("lsd,lse->de", normed_one, d_projected, preferred_element_type=F32)
-    column_sums = jnp.sum(d_projected.astype(F32), axis=(0, 1))
-    g_query_value = jnp.concatenate([column_sums[:D], column_sums[2 * D :]])
-    d_norm_one = jnp.einsum("lse,de->lsd", d_projected, w_attend, preferred_element_type=F32)
-    _, norm_back = jax.vjp(modulate_norm, tokens_float, shift_one, scale_one)
-    d_in_norm, d_shift_one, d_scale_one = norm_back(d_norm_one)
-    grad_work = d_middle + d_in_norm
-    d_modulation = jnp.concatenate(
-        [
-            d_shift_one[:, 0],
-            d_scale_one[:, 0],
-            d_gate_one,
-            d_shift_two[:, 0],
-            d_scale_two[:, 0],
-            d_gate_two,
-        ],
-        axis=-1,
-    ).astype(BF16)
+    tokens_out, grad_work, d_modulation, grads, bias_all = block_all(
+        tokens_in, cotangent, modulation[:, None, :],
+        [b[None] for b in (full_bias, b_output, b_expand, b_shrink)],
+        (w_attend, w_output, widening_matrix, narrowing_matrix),
+    )
+    d_modulation = d_modulation[:, 0].astype(BF16)
+    bias_all = bias_all[0].astype(BF16)
     return finish(
         rank, replicas, latents, local_len, cond_float, cond_act_all, modulate_weight, tokens_out,
-        grad_work, d_modulation, g_attend_w, g_query_value, g_output_w, g_output_b, g_expand_w,
-        g_expand_b, g_shrink_w, g_shrink_b,
+        grad_work, d_modulation, grads, bias_all,
     )
 
 
 def finish(
     rank, replicas, latents, local_len, cond_float, cond_act_all, modulate_weight, tokens_out,
-    grad_work, d_modulation, g_attend_w, g_query_value, g_output_w, g_output_b, g_expand_w,
-    g_expand_b, g_shrink_w, g_shrink_b,
+    grad_work, d_modulation, grads, bias_all,
 ):
     def in_order(own, other):
         return jnp.where(rank == 0, jnp.concatenate([own, other]), jnp.concatenate([other, own]))
@@ -480,11 +580,7 @@
         other = lax.ppermute(away.astype(BF16), "shard", SWAP).astype(values.dtype)
         return in_order(own, other)
 
-    grads = jnp.concatenate(
-        [in_halves(g.astype(BF16)) for g in (g_shrink_w, g_expand_w, g_attend_w, g_output_w)], axis=1
-    )
     own_cond = lax.dynamic_slice_in_dim(cond_act_all, rank * latents, latents, 0)
-    bias_all = jnp.concatenate([g_query_value, g_output_b, g_expand_b, g_shrink_b]).astype(BF16)
     flat = jnp.concatenate([d_modulation.reshape(-1), own_cond.reshape(-1), bias_all])
     block = jnp.pad(flat, (0, BLOCK_ROWS * 128 - flat.shape[0])).reshape(BLOCK_ROWS, 128)
     tokens_result = give_back(tokens_out)

time: 230 us -> 197 us (0.86)
  matrix products: 36.2 us -> 3.84 us
  Pallas kernels: 125 us -> 148 us
  local copies, waits for them, and re-layouts: 42.2 us -> 24.1 us
  other arithmetic: 17.5 us -> 12.5 us
    dot_general x18 -> x0, matrix products: 32.4 us -> none  [the longest x1 4.6 us: on_device(): jnp.einsum('ega,ap->egp', hidden_act, narrowing_matrix, preferred_element...]
    pallas_call x0 -> x1, Pallas kernels: none -> 23 us  [block_all(): pl.pallas_call(block_kernel, grid=(latents,), out_shape=(jax.ShapeDtypeSt...]
    unnamed x92 -> x22, local copies, waits for them, and re-layouts: 13.7 us -> 2.22 us
    reduce_sum x8 -> x0, other arithmetic: 5.15 us -> none  [the longest x2 1.51 us: modulate_norm(): variance = jnp.mean(centered * centered, axis=-1, keepdims=True)]
    reshape x4 -> x0, local copies, waits for them, and re-layouts: 4.74 us -> none  [the longest x3 4.74 us: on_device(): t.reshape(latents, seq_len, D)]
    slice x7 -> x0, local copies, waits for them, and re-layouts: 3.48 us -> none  [the longest x2 2.82 us: in_halves(): gradient[:, i:i + D].reshape(2, rows, D)]
    convert_element_type x2 -> x1, local copies, waits for them, and re-layouts: 2.54 us -> 0.03 us  [on_device(): d_modulation = d_modulation[:, 0].astype(BF16)]
  transfers between devices with their start and end apart: 4 -> 4, of which waited for: 1 -> 1; matrix products, arithmetic and copies ran while one was open for 18% -> 13% of each run, Pallas kernels for 24% -> 28%
where the time goes in v2:
time: 197 us; the launch traced here: 196 us
  Pallas kernels  148 us (75%)
  local copies, waits for them, and re-layouts  24.1 us (12%)
  other arithmetic  12.5 us (6%)
  starting transfers between devices  5.16 us (3%)
  matrix products  3.84 us (2%)
    pallas_call x1, Pallas kernels, gather_all(): pl.pallas_call(gather_kernel, out_shape=(tokens, tokens, jax.ShapeDtypeSt...  70 us
    pallas_call x1, Pallas kernels, reduce_all(): pl.pallas_call(functools.partial(reduce_kernel, bits), out_shape=(jax.Sha...  54.9 us
    pallas_call x1, Pallas kernels, block_all(): pl.pallas_call(block_kernel, grid=(latents,), out_shape=(jax.ShapeDtypeSt...  23 us
    dynamic_slice x3, local copies, waits for them, and re-layouts, own_bias(): lax.dynamic_slice_in_dim(bias_sum, start + rank * (size // 2), size // 2, 0)  4.05 us
  transfers between devices with their start and end apart: 4, of which 1 were waited for; matrix products, arithmetic and copies ran while one was open for 13% of the time, Pallas kernels for 28%

profile of v2, /device:TPU:0, one launch (start us, length us, event | category | flops | bytes accessed | tf_op | source)
XLA Modules:
  0.0 196.0 jit_solution(6066113353530947814)
XLA Ops:
  0.7 3.6 %concatenate.136 = bf16[2688]{0:T(1024)(128)(2,1)S(1)} concatenate(bf16[1152]{0:T(1024)(128)(2,1)} %param.17, bf16[384]{0:T(512)(128)(2,1)} %param.19, bf16[192]{0:T(256)(128)(2,1)} %param.21, bf16[768]{0:T(1024)(128)(2,1)} %param.23, bf16[192]{0:T(256)(128)(2,1)} %param.25), dimensions={0} | concatenate | bytes 10752 | tf_op jit(solution)/shard_map/concatenate | solution.py:527
  4.2 0.1 fusion.28
  4.3 0.7 fusion.19
  5.0 0.3 fusion.23
  5.4 0.6 fusion.3.small
  6.0 70.0 %shard_map.228 = (bf16[2,256,384]{2,1,0:T(8,128)(2,1)}, bf16[2,256,384]{2,1,0:T(8,128)(2,1)}, f32[64,128]{1,0:T(8,128)}, bf16[384,1152]{1,0:T(8,128)(2,1)}, bf16...) custom-call(bf16[4,128,384]{2,1,0:T(8,128)(2,1)} %tok.1, bf16[4,128,384]{2,1,0:T(8,128)(2,1)} %cot.1, ...), custom_call_target="tpu_custom_call" | custom-call | tf_op jit(solution)/shard_map/pallas_call | solution.py:149
  76.0 0.7 slice_bitcast_fusion
  76.7 0.7 slice_bitcast_fusion.2
  77.4 0.7 slice_bitcast_fusion.1
  78.1 0.7 slice.88
  78.8 0.1 fusion.27
  78.9 0.1 slice.121
  79.0 0.1 slice.120
  79.1 0.6 broadcast_in_dim.15.b_attend
  79.8 0.6 broadcast_in_dim.6.mod
  80.4 0.6 broadcast_select_fusion.b_expand
  81.0 0.6 broadcast_select_fusion.1
  81.6 23.0 %shard_map.229 = (bf16[2,256,384]{2,1,0:T(8,128)(2,1)}, f32[2,256,384]{2,1,0:T(8,128)}, f32[2,1,2304]{2,1,0:T(1,128)}, bf16[2,2304,384]{2,1,0:T(8,128)(2,1)}, f32[1,3072]{1,0:T(1,128)}) custom-call(bf16[2,256,384]{2,1,0:T(8,128)(2,1)} %get-tuple-element.27.tok, bf16[2,256,384]{2,1,0:T(8,128)(2,1)} %get-tuple-element.28.cot, ...), custom_call_target="tpu_custom_call" | custom-call | flops 5435817984 | bytes 12582912 | tf_op jit(solution)/shard_map/pallas_call | solution.py:481
  104.7 0.8 convert_element_type.49
  105.5 1.6 collective-permute-start.2
  107.1 1.7 dynamic-slice_convert_fusion
  108.7 0.5 collective-permute-start.1
  109.3 1.7 constant_dynamic-slice_fusion.3
  111.0 1.5 collective-permute-start
  112.7 2.0 %copy-done.1 = bf16[2,2304,384]{2,1,0:T(8,128)(2,1)S(1)} copy-done((bf16[2,2304,384]{2,1,0:T(8,128)(2,1)S(1)}, bf16[2,2304,384]{2,1,0:T(8,128)(2,1)}, u32[]{:S(2)}) %copy-start.1) | copy-done | bytes 3538968
  114.7 54.9 %shard_map.230 = (bf16[2304,384]{1,0:T(8,128)(2,1)S(1)}, bf16[32,80,128]{2,1,0:T(8,128)(2,1)S(1)}) custom-call(bf16[2,2304,384]{2,1,0:T(8,128)(2,1)S(1)} %copy-done.1, bf16[80,128]{1,0:T(8,128)(2,1)S(1)} %fusion.8.block), custom_call_target="tpu_custom_call" | custom-call | tf_op jit(solution)/shard_map/pallas_call | solution.py:281
  169.6 0.2 copy.30
  169.8 0.7 slice.125
  170.6 0.6 slice.124
  171.2 0.6 convert_reduce_fusion
  171.9 1.4 fusion.25
  173.3 1.1 reshape.264
  174.3 1.4 reshape.263
  175.8 2.5 %fusion.4 = f32[192,2304]{1,0:T(8,128)} fusion(bf16[64,2304]{1,0:T(8,128)(2,1)S(1)} %reshape.264, bf16[64,384]{1,0:T(8,128)(2,1)} %reshape.263, s32[]{:T(128)S(6)} %select_n.126), kind=kOutput, calls=%fused_computation.15 | convolution fusion | flops 56623104 | bytes 2097156 | tf_op jit(solution)/shard_map/lr,le->re/dot_general | solution.py:608
  178.3 2.2 %pad_maximum_fusion.1 = f32[192,1152]{1,0:T(8,128)} fusion(f32[192,384]{1,0:T(8,128)} %get-tuple-element.48, f32[192,384]{1,0:T(8,128)} %get-tuple-element.47, f32[192,384]{1,0:T(8,128)} %get-tuple-element.46), kind=kLoop, calls=%fused_computation.1 | loop fusion | flops 442368 | bytes 1769472 | tf_op jit(solution)/shard_map/concatenate | solution.py:619
  180.5 1.1 pad_maximum_fusion
  181.7 1.3 fusion.26
  183.0 1.1 slice.135
  184.1 1.4 dynamic_slice.54
  185.5 1.3 dynamic_slice.52
  186.8 1.1 fusion.9
  187.9 1.6 collective-permute-start.3
  189.4 0.6 convert_reduce_fusion.1
  190.1 1.5 collective-permute-done.3
  191.6 0.7 fusion.21
  192.2 1.0 convert_element_type.48
  193.2 0.9 maximum_select_fusion
  194.1 1.8 maximum_select_fusion.1
  (44 shorter events, 0.4 us)
Async XLA Ops:
  0.6 4.4 %copy-start = (bf16[192,2304]{1,0:T(8,128)(2,1)S(1)}, bf16[192,2304]{1,0:T(8,128)(2,1)}, u32[]{:S(2)}) copy-start(bf16[192,2304]{1,0:T(8,128)(2,1)} %param.16) | copy-start | bytes 2654212
  104.7 7.8 %copy-start.7 = (f32[2,1,2304]{2,1,0:T(1,128)S(1)}, f32[2,1,2304]{2,1,0:T(1,128)}, u32[]{:S(2)}) copy-start(f32[2,1,2304]{2,1,0:T(1,128)} %get-tuple-element.36) | copy-start | bytes 55300
  104.7 7.9 %copy-start.9 = (f32[1,3072]{1,0:T(1,128)S(1)}, f32[1,3072]{1,0:T(1,128)}, u32[]{:S(2)}) copy-start(f32[1,3072]{1,0:T(1,128)} %get-tuple-element.38) | copy-start | bytes 36868
  105.5 81.3 %collective-permute-start.2 = (bf16[2,2304]{1,0:T(2,128)(2,1)S(1)}, bf16[2,2304]{1,0:T(2,128)(2,1)}, u32[]{:S(2)}, u32[]{:S(2)}) collective-permute-start(bf16[2,2304]{1,0:T(2,128)(2,1)S(1)} %bitcast.28), channel_id=1, source_target_pairs={{0,1},{1,0},{2,3},{3,2},{4,5},{5,4},{6,7},{7,6},{8,9},{9,8},{10,11... | collective-permute-start | bytes 27656 | tf_op jit(solution)/shard_map/ppermute | solution.py:588
  108.7 83.5 %collective-permute-start.1 = (bf16[2,128,384]{2,1,0:T(8,128)(2,1)}, bf16[2,128,384]{2,1,0:T(8,128)(2,1)}, u32[]{:S(2)}, u32[]{:S(2)}) collective-permute-start(bf16[2,128,384]{2,1,0:T(8,128)(2,1)} %dynamic-slice_convert_fusion), channel_id=1, source_target_pairs={{0,1},{1,0},{2,3},{3,2},{4,5},{5,4},{6,7},{7,6},{8,9},{9,8},{10,11... | collective-permute-start | bytes 589832 | tf_op jit(solution)/shard_map/ppermute | solution.py:580
  111.0 83.1 %collective-permute-start = (bf16[2,128,384]{2,1,0:T(8,128)(2,1)}, bf16[2,128,384]{2,1,0:T(8,128)(2,1)}, u32[]{:S(2)}, u32[]{:S(2)}) collective-permute-start(bf16[2,128,384]{2,1,0:T(8,128)(2,1)} %get-tuple-element.50), channel_id=1, source_target_pairs={{0,1},{1,0},{2,3},{3,2},{4,5},{5,4},{6,7},{7,6},{8,9},{9,8},{10,11... | collective-permute-start | bytes 589832 | tf_op jit(solution)/shard_map/ppermute | solution.py:580
  112.7 2.0 %copy-start.1 = (bf16[2,2304,384]{2,1,0:T(8,128)(2,1)S(1)}, bf16[2,2304,384]{2,1,0:T(8,128)(2,1)}, u32[]{:S(2)}) copy-start(bf16[2,2304,384]{2,1,0:T(8,128)(2,1)} %get-tuple-element.37.grads) | copy-start | bytes 10616836
  169.6 2.2 %copy-start.6 = (f32[2,256,384]{2,1,0:T(8,128)S(1)}, f32[2,256,384]{2,1,0:T(8,128)}, u32[]{:S(2)}) copy-start(f32[2,256,384]{2,1,0:T(8,128)} %get-tuple-element.35) | copy-start | bytes 2359300
  178.3 2.2 %copy-start.2 = (f32[192,384]{1,0:T(8,128)S(1)}, f32[192,384]{1,0:T(8,128)}, u32[]{:S(2)}) copy-start(f32[192,384]{1,0:T(8,128)} %get-tuple-element.41) | copy-start | bytes 884740
  178.3 2.2 %copy-start.3 = (f32[192,384]{1,0:T(8,128)S(1)}, f32[192,384]{1,0:T(8,128)}, u32[]{:S(2)}) copy-start(f32[192,384]{1,0:T(8,128)} %get-tuple-element.42) | copy-start | bytes 884740
  178.3 2.2 %copy-start.4 = (f32[192,384]{1,0:T(8,128)S(1)}, f32[192,384]{1,0:T(8,128)}, u32[]{:S(2)}) copy-start(f32[192,384]{1,0:T(8,128)} %get-tuple-element.43) | copy-start | bytes 884740
  178.3 2.2 %copy-start.5 = (f32[192,384]{1,0:T(8,128)S(1)}, f32[192,384]{1,0:T(8,128)}, u32[]{:S(2)}) copy-start(f32[192,384]{1,0:T(8,128)} %get-tuple-element.44) | copy-start | bytes 884740
  183.0 8.6 %copy-start.8 = (bf16[4,384]{1,0:T(4,128)(2,1)S(1)}, bf16[4,384]{1,0:T(4,128)(2,1)}, u32[]{:S(2)}) copy-start(bf16[4,384]{1,0:T(4,128)(2,1)} %param.14) | copy-start | bytes 9220
  187.9 3.7 %collective-permute-start.3 = (f32[4,192]{1,0:T(4,128)S(1)}, f32[4,192]{1,0:T(4,128)S(1)}, u32[]{:S(2)}, u32[]{:S(2)}) collective-permute-start(f32[4,192]{1,0:T(4,128)S(1)} %fusion.9), channel_id=1, source_target_pairs={{0,1},{1,0},{2,3},{3,2},{4,5},{5,4},{6,7},{7,6},{8,9},{9,8},{10,11... | collective-permute-start | bytes 9224 | tf_op jit(solution)/shard_map/ppermute | solution.py:592

commit v3 on v2

--- a/solution.py
+++ b/solution.py
@@ -37,7 +37,7 @@
 def gather_kernel(
     tok, cot, small, wa, wo, ww, wn,
     tok_all, cot_all, small_other, wa_all, wo_all, ww_all, wn_all,
-    send_one, recv_one, send_w, recv_w, local_sem,
+    send_one, recv_one, send_w, recv_w,
 ):
     r, s = lax.axis_index("replica"), lax.axis_index("shard")
     o = 1 - s
@@ -86,18 +86,11 @@
         )
     first[0].start()
     first[1].start()
-    locals_ = []
-    for k, (src, dst) in enumerate(((tok, tok_all), (cot, cot_all))):
-        locals_.append(
-            pltpu.make_async_copy(src.at[pl.ds(s * group, group)], dst.at[:, place], local_sem.at[k])
-        )
-    for k, (own, full) in enumerate(pairs):
+    tok_all[:, place] = tok[pl.ds(s * group, group)]
+    cot_all[:, place] = cot[pl.ds(s * group, group)]
+    for own, full in pairs:
         n = own.shape[0]
-        locals_.append(
-            pltpu.make_async_copy(own, full.at[pl.ds(pl.multiple_of(s * n, n), n)], local_sem.at[2 + k])
-        )
-    for c in locals_:
-        c.start()
+        full[pl.ds(pl.multiple_of(s * n, n), n)] = own[...]
     later = []
 
     def forward(k):
@@ -129,8 +122,6 @@
         last[k].wait_recv()
     for c in (swaps[0], swaps[2]):
         c.wait_recv()
-    for c in locals_:
-        c.wait()
     for c in swaps + first + last:
         c.wait_send()
     for a, b in later:
@@ -139,7 +130,7 @@
 
 
 def gather_all(tok, cot, small, wa, wo, ww, wn):
-    any_spec = pl.BlockSpec(memory_space=pl.ANY)
+    vmem = pl.BlockSpec(memory_space=pltpu.VMEM)
     group = tok.shape[0] // 2
 
     def full(w):
@@ -152,16 +143,17 @@
             tokens, tokens, jax.ShapeDtypeStruct(small.shape, small.dtype),
             full(wa), full(wo), full(ww), full(wn),
         ),
-        in_specs=[any_spec] * 7,
-        out_specs=(any_spec,) * 7,
+        in_specs=[vmem] * 7,
+        out_specs=(vmem,) * 7,
         scratch_shapes=[
             pltpu.SemaphoreType.DMA((3,)),
             pltpu.SemaphoreType.DMA((3,)),
             pltpu.SemaphoreType.DMA((4, 4)),
             pltpu.SemaphoreType.DMA((4, 4)),
-            pltpu.SemaphoreType.DMA((6,)),
         ],
-        compiler_params=pltpu.CompilerParams(collective_id=0, has_side_effects=True),
+        compiler_params=pltpu.CompilerParams(
+            collective_id=0, has_side_effects=True, vmem_limit_bytes=48 * 2**20
+        ),
     )(tok, cot, small, wa, wo, ww, wn)
 
 
@@ -261,11 +253,13 @@
             spot = spot - bit_of(r, k) * n
             n *= 2
 
-    waiting = [chunk_steps(j) for j in range(CHUNKS)]
+    chunks = [chunk_steps(j) for j in range(CHUNKS)]
+    for steps in chunks:
+        next(steps)
     running = [gather_steps()]
-    while running or waiting:
-        if waiting:
-            running.append(waiting.pop(0))
+    while running or chunks:
+        if chunks:
+            running.insert(0, chunks.pop(0))
         for steps in list(running):
             if next(steps, 0) == 0:
                 running.remove(steps)
@@ -498,6 +492,63 @@
     )(tok, cot, mod, *shared)
 
 
+def unpack_kernel(
+    latents, reduced, blocks, g_mod_w, g_mod_b, attend, g_qv, g_out_w, g_out_b, expand, g_exp_b, shrink,
+    g_shr_b, wide,
+):
+    first = lax.axis_index("shard") == 0
+    half = D // 2
+    wide[...] = blocks[...].astype(F32)
+    shrink[...] = reduced[0:ROWS].astype(F32)
+    for i in range(4):
+        expand[:, i * D : (i + 1) * D] = reduced[ROWS + i * half : ROWS + (i + 1) * half].astype(F32)
+    for i in range(3):
+        attend[:, i * D : (i + 1) * D] = reduced[
+            2 * ROWS + i * half : 2 * ROWS + (i + 1) * half
+        ].astype(F32)
+    g_out_w[...] = reduced[2 * ROWS + 3 * half :].astype(F32)
+
+    def lines(start, count):
+        return jnp.concatenate([wide[:, i, :] for i in range(start, start + count)], axis=1)
+
+    n_mod, n_act = 6 * D // 128, D // 128
+    mods = jnp.concatenate([lines(k * n_mod, n_mod) for k in range(latents)], axis=0)
+    acts = jnp.concatenate(
+        [lines(latents * n_mod + k * n_act, n_act) for k in range(latents)], axis=0
+    )
+    own = jnp.where(first, acts[:, :half], acts[:, half:]).astype(BF16)
+    low = mods.astype(BF16)
+    for i in range(6):
+        cols = slice(i * D, (i + 1) * D)
+        g_mod_w[:, cols] = dot_tn(own, low[:, cols])
+    sums = row_sum(mods)
+    g_mod_b[...] = jnp.where(first, sums[:, : 3 * D], sums[:, 3 * D :])
+    bias = row_sum(lines(latents * (n_mod + n_act), (4 * D + FF) // 128))
+    start = 0
+    for ref in (g_qv, g_out_b, g_exp_b, g_shr_b):
+        n = ref.shape[1]
+        ref[...] = jnp.where(first, bias[:, start : start + n], bias[:, start + n : start + 2 * n])
+        start += 2 * n
+
+
+def unpack_all(reduced, blocks, latents):
+    vmem = pl.BlockSpec(memory_space=pltpu.VMEM)
+    half = D // 2
+    shapes = [
+        (half, 6 * D), (1, 3 * D), (half, 3 * D), (1, D), (half, D), (1, half), (half, FF), (1, FF // 2),
+        (FF // 2, D), (1, half),
+    ]
+    return pl.pallas_call(
+        functools.partial(unpack_kernel, latents),
+        out_shape=[jax.ShapeDtypeStruct(n, F32) for n in shapes],
+        in_specs=[vmem, vmem],
+        out_specs=[vmem] * len(shapes),
+        scratch_shapes=[pltpu.VMEM(blocks.shape, F32)],
+        compiler_params=pltpu.CompilerParams(vmem_limit_bytes=56 * 2**20),
+        cost_estimate=pl.CostEstimate(flops=2**26, bytes_accessed=8 * 2**20, transcendentals=0),
+    )(reduced, blocks)
+
+
 def on_device(
     tokens_in,
     condition,
@@ -599,38 +650,23 @@
     grad_condition = silu_back(d_cond)[0]
 
     reduced, blocks = reduce_all(grads, block, replicas)
-    flat_blocks = blocks.reshape(2 * replicas, BLOCK_ROWS * 128)
-    n_mod, n_cond = latents * 6 * D, latents * D
-    d_mod_all = flat_blocks[:, :n_mod].reshape(-1, 6 * D)
-    act_all = flat_blocks[:, n_mod : n_mod + n_cond].reshape(-1, D)
-    bias_sum = jnp.sum(flat_blocks[:, n_mod + n_cond : n_mod + n_cond + bias_all.shape[0]].astype(F32), axis=0)
-    own_act = lax.dynamic_slice_in_dim(act_all, rank * (D // 2), D // 2, 1)
-    g_modulate_w = jnp.einsum("lr,le->re", own_act, d_mod_all, preferred_element_type=F32)
-    g_modulate_b = jnp.sum(
-        lax.dynamic_slice_in_dim(d_mod_all, rank * 3 * D, 3 * D, 1).astype(F32), axis=0
-    )
-
-    def own_bias(start, size):
-        return lax.dynamic_slice_in_dim(bias_sum, start + rank * (size // 2), size // 2, 0)
-
-    reduced = reduced.astype(F32)
-    half = D // 2
-    expand = jnp.concatenate([reduced[768 + i * half : 768 + (i + 1) * half] for i in range(4)], axis=1)
-    attend = jnp.concatenate([reduced[1536 + i * half : 1536 + (i + 1) * half] for i in range(3)], axis=1)
+    g_mod_w, g_mod_b, attend, g_qv, g_out_w, g_out_b, expand, g_exp_b, shrink, g_shr_b = unpack_all(
+        reduced, blocks, latents
+    )
     return (
         tokens_result,
         grad_result,
         grad_condition,
-        g_modulate_w,
-        g_modulate_b,
+        g_mod_w,
+        g_mod_b[0],
         attend,
-        own_bias(0, 2 * D),
-        reduced[1536 + 3 * half :],
-        own_bias(2 * D, D),
+        g_qv[0],
+        g_out_w,
+        g_out_b[0],
         expand,
-        own_bias(3 * D, FF),
-        reduced[:768],
-        own_bias(3 * D + FF, D),
+        g_exp_b[0],
+        shrink,
+        g_shr_b[0],
     )
 
 

time: 197 us -> 142 us (0.72)
  Pallas kernels: 148 us -> 106 us
  local copies, waits for them, and re-layouts: 24.1 us -> 19.6 us
  matrix products: 3.84 us -> 0.57 us
  other arithmetic: 12.5 us -> 9.24 us
    pallas_call x1, Pallas kernels: 70 us -> 26.4 us  [gather_all(): pl.pallas_call(gather_kernel, out_shape=(tokens, tokens, jax.ShapeDtypeSt...]
    unnamed x22 -> x39, local copies, waits for them, and re-layouts: 2.22 us -> 12.2 us
    pallas_call x0 -> x1, Pallas kernels: none -> 4.7 us  [unpack_all(): pl.pallas_call(functools.partial(unpack_kernel, latents), out_shape=[jax....]
    dynamic_slice x3 -> x0, local copies, waits for them, and re-layouts: 4.05 us -> none  [own_bias(): lax.dynamic_slice_in_dim(bias_sum, start + rank * (size // 2), size // 2, 0)]
    pallas_call x0 -> x3, other arithmetic: none -> 3.87 us  [unpack_all(): pl.pallas_call(functools.partial(unpack_kernel, latents), out_shape=[jax....]
    slice x4 -> x0, local copies, waits for them, and re-layouts: 3.86 us -> none  [the longest x1 1.41 us: finish(): reduced[768 + i * half:768 + (i + 1) * half]]
    concatenate x2 -> x0, other arithmetic: 3.35 us -> none  [the longest x1 2.2 us: finish(): jnp.concatenate([reduced[1536 + i * half:1536 + (i + 1) * half] for i in...]
    pallas_call x1, Pallas kernels: 54.9 us -> 51.8 us  [reduce_all(): pl.pallas_call(functools.partial(reduce_kernel, bits), out_shape=(jax.Sha...]
  transfers between devices with their start and end apart: 4 -> 4, of which waited for: 1 -> 0; matrix products, arithmetic and copies ran while one was open for 13% -> 6% of each run, Pallas kernels for 28% -> 40%
where the time goes in v3:
time: 142 us; the launch traced here: 141 us
  Pallas kernels  106 us (75%)
  local copies, waits for them, and re-layouts  19.6 us (14%)
  other arithmetic  9.24 us (7%)
  starting transfers between devices  4.99 us (4%)
    pallas_call x1, Pallas kernels, reduce_all(): pl.pallas_call(functools.partial(reduce_kernel, bits), out_shape=(jax.Sha...  51.8 us
    pallas_call x1, Pallas kernels, gather_all(): pl.pallas_call(gather_kernel, out_shape=(tokens, tokens, jax.ShapeDtypeSt...  26.4 us
    pallas_call x1, Pallas kernels, block_all(): pl.pallas_call(block_kernel, grid=(latents,), out_shape=(jax.ShapeDtypeSt...  23 us
    unnamed x39, local copies, waits for them, and re-layouts  12.2 us
    pallas_call x1, Pallas kernels, unpack_all(): pl.pallas_call(functools.partial(unpack_kernel, latents), out_shape=[jax....  4.7 us
    pallas_call x3, other arithmetic, unpack_all(): pl.pallas_call(functools.partial(unpack_kernel, latents), out_shape=[jax....  3.87 us
    concatenate x1, local copies, waits for them, and re-layouts, on_device(): jnp.concatenate([modulate_bias, query_value_bias, output_bias, widening_b...  3.61 us
  transfers between devices with their start and end apart: 4, of which 0 were waited for; matrix products, arithmetic and copies ran while one was open for 6% of the time, Pallas kernels for 40%

profile of v3, /device:TPU:0, one launch (start us, length us, event | category | flops | bytes accessed | tf_op | source)
XLA Modules:
  0.0 141.2 jit_solution(10420702878146167696)
XLA Ops:
  0.6 0.0 copy-start
  0.7 3.6 %concatenate.130 = bf16[2688]{0:T(1024)(128)(2,1)S(1)} concatenate(bf16[1152]{0:T(1024)(128)(2,1)} %param.17, bf16[384]{0:T(512)(128)(2,1)} %param.19, bf16[192]{0:T(256)(128)(2,1)} %param.21, bf16[768]{0:T(1024)(128)(2,1)} %param.23, bf16[192]{0:T(256)(128)(2,1)} %param.25), dimensions={0} | concatenate | bytes 10752 | tf_op jit(solution)/shard_map/concatenate | solution.py:578
  4.3 0.1 fusion.25
  4.4 0.1 slice.72
  4.5 0.7 fusion.17
  5.2 0.3 fusion.20
  5.5 0.0 copy-start.5
  5.6 1.1 copy-done.5
  6.6 1.0 copy-done.7
  7.6 1.0 copy-done.8
  8.6 0.9 copy-done.9
  9.5 26.4 %shard_map.228 = (bf16[2,256,384]{2,1,0:T(8,128)(2,1)S(1)}, bf16[2,256,384]{2,1,0:T(8,128)(2,1)S(1)}, f32[64,128]{1,0:T(8,128)S(1)}, bf16[384,1152]{1,0:T(8,128)...) custom-call(bf16[4,128,384]{2,1,0:T(8,128)(2,1)S(1)} %copy-done.7, ...), custom_call_target="tpu_custom_call" | custom-call | tf_op jit(solution)/shard_map/pallas_call | solution.py:140
  35.9 0.0 copy-start.10
  35.9 1.0 copy-done.10
  36.9 0.9 copy-done.11
  37.8 0.7 copy-done.12
  38.6 0.7 copy-done.13
  39.3 0.7 copy-done.14
  40.1 0.1 fusion.24
  40.1 0.1 slice.73
  40.3 0.6 broadcast_in_dim.15.b_attend
  40.9 0.6 broadcast_in_dim.6.mod
  41.5 0.6 broadcast_select_fusion.b_expand
  42.1 0.6 broadcast_select_fusion.1
  42.8 23.0 %shard_map.229 = (bf16[2,256,384]{2,1,0:T(8,128)(2,1)}, f32[2,256,384]{2,1,0:T(8,128)}, f32[2,1,2304]{2,1,0:T(1,128)}, bf16[2,2304,384]{2,1,0:T(8,128)(2,1)}, f32[1,3072]{1,0:T(1,128)}) custom-call(bf16[2,256,384]{2,1,0:T(8,128)(2,1)} %copy-done.12, bf16[2,256,384]{2,1,0:T(8,128)(2,1)} %copy-done.13, f32[2,1,2304]{2,1,0:T(1,128)} %broadcast_in_dim.6.mod, ...), custom_call_target="tpu_custom_call" | custom-call | flops 5435817984 | bytes 12582912 | tf_op jit(solution)/shard_map/pallas_call | solution.py:475
  65.8 0.0 copy-start.15
  65.8 0.8 convert_element_type.40
  66.7 1.6 %collective-permute-start.2 = (bf16[2,2304]{1,0:T(2,128)(2,1)S(1)}, bf16[2,2304]{1,0:T(2,128)(2,1)S(1)}, u32[]{:S(2)}, u32[]{:S(2)}) collective-permute-start(bf16[2,2304]{1,0:T(2,128)(2,1)S(1)} %bitcast.21), channel_id=1, source_target_pairs={{0,1},{1,0},{2,3},{3,2},{4,5},{5,4},{6,7},{7,6},{8,9},{9,8},{10,11... | collective-permute-start | bytes 27656 | tf_op jit(solution)/shard_map/ppermute | solution.py:639
  68.3 1.0 dynamic-slice_convert_fusion
  69.3 0.5 collective-permute-start.1
  69.9 1.1 constant_dynamic-slice_fusion.3
  70.9 1.6 %collective-permute-start = (bf16[2,128,384]{2,1,0:T(8,128)(2,1)S(1)}, bf16[2,128,384]{2,1,0:T(8,128)(2,1)S(1)}, u32[]{:S(2)}, u32[]{:S(2)}) collective-permute-start(bf16[2,128,384]{2,1,0:T(8,128)(2,1)S(1)} %get-tuple-element.62), channel_id=1, source_target_pairs={{0,1},{1,0},{2,3},{3,2},{4,5},{5,4},{6,7},{7,6},{8,9},{9,8},{10,11... | collective-permute-start | bytes 589832 | tf_op jit(solution)/shard_map/ppermute | solution.py:631
  72.6 0.1 convert_reduce_fusion.1
  72.8 2.0 %copy-done.1 = bf16[2,2304,384]{2,1,0:T(8,128)(2,1)S(1)} copy-done((bf16[2,2304,384]{2,1,0:T(8,128)(2,1)S(1)}, bf16[2,2304,384]{2,1,0:T(8,128)(2,1)}, u32[]{:S(2)}) %copy-start.1) | copy-done | bytes 3538968
  74.8 51.8 %shard_map.230 = (bf16[2304,384]{1,0:T(8,128)(2,1)S(1)}, bf16[32,80,128]{2,1,0:T(8,128)(2,1)S(1)}) custom-call(bf16[2,2304,384]{2,1,0:T(8,128)(2,1)S(1)} %copy-done.1, bf16[80,128]{1,0:T(8,128)(2,1)S(1)} %fusion.6.block), custom_call_target="tpu_custom_call" | custom-call | tf_op jit(solution)/shard_map/pallas_call | solution.py:275
  126.7 1.2 copy-done.2
  127.9 0.8 copy-done.3
  128.7 0.3 fusion.7
  129.0 1.2 collective-permute-start.3
  130.2 4.7 %shard_map.231 = (f32[192,2304]{1,0:T(8,128)}, f32[1,1152]{1,0:T(1,128)}, f32[192,1152]{1,0:T(8,128)}, f32[1,384]{1,0:T(1,128)}, f32[192,384]{1,0:T(8,128)}, /*i...) custom-call(bf16[2304,384]{1,0:T(8,128)(2,1)} %copy-done.2, ...), custom_call_target="tpu_custom_call" | custom-call | flops 67108864 | bytes 8388608 | tf_op jit(solution)/shard_map/pallas_call | solution.py:541
  134.9 1.3 reduce.3
  136.2 1.3 reduce.4
  137.5 1.3 reduce.2
  138.8 0.7 fusion.19
  139.5 0.0 collective-permute-done.1
  139.5 0.9 maximum_select_fusion
  140.4 0.0 collective-permute-done
  140.4 0.8 maximum_select_fusion.1
  (51 shorter events, 0.4 us)
Async XLA Ops:
  0.6 4.5 %copy-start = (bf16[192,2304]{1,0:T(8,128)(2,1)S(1)}, bf16[192,2304]{1,0:T(8,128)(2,1)}, u32[]{:S(2)}) copy-start(bf16[192,2304]{1,0:T(8,128)(2,1)} %param.16) | copy-start | bytes 2654212
  0.7 4.9 %copy-start.4 = (bf16[192,1536]{1,0:T(8,128)(2,1)S(1)}, bf16[192,1536]{1,0:T(8,128)(2,1)}, u32[]{:S(2)}) copy-start(bf16[192,1536]{1,0:T(8,128)(2,1)} %ww.1) | copy-start | bytes 1769476
  0.7 4.9 %copy-start.6 = (bf16[192,1152]{1,0:T(8,128)(2,1)S(1)}, bf16[192,1152]{1,0:T(8,128)(2,1)}, u32[]{:S(2)}) copy-start(bf16[192,1152]{1,0:T(8,128)(2,1)} %wa.1) | copy-start | bytes 1327108
  5.5 1.1 copy-start.5
  6.6 1.0 copy-start.7
  7.6 1.0 copy-start.8
  8.6 0.9 copy-start.9
  35.9 1.0 copy-start.10
  36.9 0.9 copy-start.11
  37.8 0.7 copy-start.12
  38.6 0.7 copy-start.13
  39.3 0.7 copy-start.14
  65.8 6.8 %copy-start.16 = (f32[2,1,2304]{2,1,0:T(1,128)S(1)}, f32[2,1,2304]{2,1,0:T(1,128)}, u32[]{:S(2)}) copy-start(f32[2,1,2304]{2,1,0:T(1,128)} %get-tuple-element.46) | copy-start | bytes 55300
  65.8 6.8 %copy-start.15 = (f32[2,256,384]{2,1,0:T(8,128)S(1)}, f32[2,256,384]{2,1,0:T(8,128)}, u32[]{:S(2)}) copy-start(f32[2,256,384]{2,1,0:T(8,128)} %get-tuple-element.45) | copy-start | bytes 2359300
  65.8 6.9 %copy-start.18 = (f32[1,3072]{1,0:T(1,128)S(1)}, f32[1,3072]{1,0:T(1,128)}, u32[]{:S(2)}) copy-start(f32[1,3072]{1,0:T(1,128)} %get-tuple-element.48) | copy-start | bytes 36868
  66.7 62.1 %collective-permute-start.2 = (bf16[2,2304]{1,0:T(2,128)(2,1)S(1)}, bf16[2,2304]{1,0:T(2,128)(2,1)S(1)}, u32[]{:S(2)}, u32[]{:S(2)}) collective-permute-start(bf16[2,2304]{1,0:T(2,128)(2,1)S(1)} %bitcast.21), channel_id=1, source_target_pairs={{0,1},{1,0},{2,3},{3,2},{4,5},{5,4},{6,7},{7,6},{8,9},{9,8},{10,11... | collective-permute-start | bytes 27656 | tf_op jit(solution)/shard_map/ppermute | solution.py:639
  69.3 70.1 %collective-permute-start.1 = (bf16[2,128,384]{2,1,0:T(8,128)(2,1)S(1)}, bf16[2,128,384]{2,1,0:T(8,128)(2,1)S(1)}, u32[]{:S(2)}, u32[]{:S(2)}) collective-permute-start(bf16[2,128,384]{2,1,0:T(8,128)(2,1)S(1)} %dynamic-slice_convert_fusion), channel_id=1, source_target_pairs={{0,1},{1,0},{2,3},{3,2},{4,5},{5,4},{6,7},{7,6},{8,9},{9,8},{10,11... | collective-permute-start | bytes 589832 | tf_op jit(solution)/shard_map/ppermute | solution.py:631
  70.9 69.5 %collective-permute-start = (bf16[2,128,384]{2,1,0:T(8,128)(2,1)S(1)}, bf16[2,128,384]{2,1,0:T(8,128)(2,1)S(1)}, u32[]{:S(2)}, u32[]{:S(2)}) collective-permute-start(bf16[2,128,384]{2,1,0:T(8,128)(2,1)S(1)} %get-tuple-element.62), channel_id=1, source_target_pairs={{0,1},{1,0},{2,3},{3,2},{4,5},{5,4},{6,7},{7,6},{8,9},{9,8},{10,11... | collective-permute-start | bytes 589832 | tf_op jit(solution)/shard_map/ppermute | solution.py:631
  72.8 2.0 %copy-start.1 = (bf16[2,2304,384]{2,1,0:T(8,128)(2,1)S(1)}, bf16[2,2304,384]{2,1,0:T(8,128)(2,1)}, u32[]{:S(2)}) copy-start(bf16[2,2304,384]{2,1,0:T(8,128)(2,1)} %get-tuple-element.47.grads) | copy-start | bytes 10616836
  126.6 1.2 copy-start.2
  127.9 0.8 copy-start.3
  129.0 9.8 %collective-permute-start.3 = (f32[4,192]{1,0:T(4,128)S(1)}, f32[4,192]{1,0:T(4,128)S(1)}, u32[]{:S(2)}, u32[]{:S(2)}) collective-permute-start(f32[4,192]{1,0:T(4,128)S(1)} %fusion.7), channel_id=1, source_target_pairs={{0,1},{1,0},{2,3},{3,2},{4,5},{5,4},{6,7},{7,6},{8,9},{9,8},{10,11... | collective-permute-start | bytes 9224 | tf_op jit(solution)/shard_map/ppermute | solution.py:643
  130.2 8.6 %copy-start.17 = (bf16[4,384]{1,0:T(4,128)(2,1)S(1)}, bf16[4,384]{1,0:T(4,128)(2,1)}, u32[]{:S(2)}) copy-start(bf16[4,384]{1,0:T(4,128)(2,1)} %param.14) | copy-start | bytes 9220
